TPU v7x, 768 devices: a whole 4x8x12 slice. The times are simulated.
768 devices in a mesh: gx: 192 (over y, z, core), gy: 4 (over x).
Axes of the slice: x: 4, y: 8, z: 12, core: 2. Of those that a mesh axis runs over, the one named last changes fastest.
Arguments:
- adjoint_source: float32 [2, 11, 1536, 512], P(None, None, 'gx', 'gy'), may hold values from -80 to 80, as said below
- viscosity: float32 [11, 1536, 512], P(None, 'gx', 'gy'), may hold values from 0.3 to 3
- friction: float32 [1536, 512], P('gx', 'gy'), may hold values from 0.1 to 10
- ice_mask: int32 [1536, 512], P('gx', 'gy'), may hold values 0 or 1
Outputs:
- adjoint_velocity: float32 [2, 11, 1536, 512], P(None, None, 'gx', 'gy')
- residual: float32 [2, 11, 1536, 512], P(None, None, 'gx', 'gy')
Inputs may be any that keep to these rules, and one draw needn't show every extreme that they name: `adjoint_source`: rough from column to column, of varying scale.
All inputs are finite; a program needn't handle non-finite values. No bound on the sum of `ice_mask` on one device may be relied on, other than what follows from the above.
Results may differ from a plain program's by a relative error of at most 0.006.
Values sent between devices are 32-bit elements; how exact they have to be, the bound alone decides.
No kernel may reach another device: no remote copies, remote signals or barrier semaphores. Data moves between devices by JAX's collectives and lax.ppermute only.
A program may use at most 32 MiB of HBM per device.

v0:
```python
import math

import jax
import jax.numpy as jnp
import numpy as np
from jax import lax
from jax.sharding import PartitionSpec as P

ITERS = 3


vertical_weight = 4.0


def extended(value, sides, width):
    for axis, dim in sides:
        size, length = (lax.axis_size(axis), value.shape[dim])
        up = [(i, (i + 1) % size) for i in range(size - 1)]
        down = [(j, i) for i, j in up]
        last = lax.slice_in_dim(value, length - width, length, axis=dim)
        initial = lax.slice_in_dim(value, 0, width, axis=dim)
        before = lax.ppermute(last, axis, up)
        after = lax.ppermute(initial, axis, down)
        value = jnp.concatenate([before, value, after], axis=dim)
    return value


def corner_offsets():
    return [
        (upper_z, upper_x, upper_y)
        for upper_z in (0, 1)
        for upper_x in (0, 1)
        for upper_y in (0, 1)
    ]


def element_table():
    gauss_points = [0.5 - 0.5 / math.sqrt(3.0), 0.5 + 0.5 / math.sqrt(3.0)]
    corner_list = corner_offsets()
    gradients = np.zeros((3, 8, 8))
    for quad_index, quad_corner in enumerate(corner_list):
        coords = [gauss_points[picked] for picked in quad_corner]
        for node_index, node_corner in enumerate(corner_list):
            factors = [
                coords[axis_index] if node_corner[axis_index] else 1.0 - coords[axis_index]
                for axis_index in range(3)
            ]
            slopes = [1.0 if node_corner[axis_index] else -1.0 for axis_index in range(3)]
            gradients[0, node_index, quad_index] = slopes[1] * factors[0] * factors[2]
            gradients[1, node_index, quad_index] = slopes[2] * factors[0] * factors[1]
            gradients[2, node_index, quad_index] = slopes[0] * factors[1] * factors[2]
    pairs = np.zeros((3, 3, 8, 8))
    for first_axis in range(3):
        for second_axis in range(3):
            for node_index in range(8):
                for other_index in range(8):
                    total = 0.0
                    for quad_index in range(8):
                        total += (
                            gradients[first_axis, node_index, quad_index]
                            * gradients[second_axis, other_index, quad_index]
                        )
                    pairs[first_axis, second_axis, node_index, other_index] = total / 8.0
    along_uu = 4.0 * pairs[0, 0] + pairs[1, 1] + vertical_weight * pairs[2, 2]
    along_vv = pairs[0, 0] + 4.0 * pairs[1, 1] + vertical_weight * pairs[2, 2]
    coupled = 2.0 * pairs[0, 1] + pairs[1, 0]
    table = np.zeros((16, 16))
    table[0:8, 0:8] = along_uu
    table[0:8, 8:16] = coupled
    table[8:16, 0:8] = np.transpose(coupled)
    table[8:16, 8:16] = along_vv
    return table.astype(np.float32)


def cell_residual(padded, eta_padded):
    layers = padded.shape[1] - 1
    cells_x = padded.shape[2] - 1
    cells_y = padded.shape[3] - 1
    corner_list = corner_offsets()
    pieces = []
    for component in (0, 1):
        for upper_z, upper_x, upper_y in corner_list:
            pieces.append(
                padded[
                    component,
                    upper_z : upper_z + layers,
                    upper_x : upper_x + cells_x,
                    upper_y : upper_y + cells_y,
                ]
            )
    stacked = jnp.stack(pieces)
    eta_cells = eta_padded[0:layers, 0:cells_x, 0:cells_y]
    for upper_z, upper_x, upper_y in corner_list[1:]:
        eta_cells = (
            eta_cells
            + eta_padded[
                upper_z : upper_z + layers, upper_x : upper_x + cells_x, upper_y : upper_y + cells_y
            ]
        )
    eta_cells = eta_cells * 0.125
    table = jnp.asarray(element_table(), dtype=padded.dtype)
    products = (
        jnp.einsum("ij,jlxy->ilxy", table, stacked, precision=lax.Precision.HIGHEST)
        * eta_cells[None]
    )
    outputs = []
    for component in (0, 1):
        summed = jnp.zeros(padded.shape[1:], padded.dtype)
        for corner_index, (upper_z, upper_x, upper_y) in enumerate(corner_list):
            summed = summed + jnp.pad(
                products[component * 8 + corner_index],
                ((upper_z, 1 - upper_z), (upper_x, 1 - upper_x), (upper_y, 1 - upper_y)),
            )
        outputs.append(summed)
    return jnp.stack(outputs)


def local(adjoint_source, viscosity, friction, ice_mask):
    eta_padded = extended(viscosity, (("gx", 1), ("gy", 2)), 1)
    weights = ice_mask.astype(adjoint_source.dtype)[None, None]
    residual = adjoint_source * weights
    adjoint_velocity = jnp.zeros_like(residual)

    def global_total(value):
        return lax.psum(lax.psum(value, "gy"), "gx")

    direction = residual
    norm_now = global_total(jnp.sum(residual * residual))
    for iteration in range(ITERS):
        padded = extended(direction, (("gx", 2), ("gy", 3)), 1)
        stiffness = cell_residual(padded, eta_padded)[:, :, 1:-1, 1:-1]
        bed_rows = stiffness[:, 0] + friction[None] * direction[:, 0]
        stiffness = stiffness.at[:, 0].set(bed_rows)
        image = stiffness * weights
        alpha = norm_now / global_total(jnp.sum(direction * image))
        adjoint_velocity = adjoint_velocity + alpha * direction
        residual = residual - alpha * image
        norm_next = global_total(jnp.sum(residual * residual))
        direction = residual + norm_next / norm_now * direction
        norm_now = norm_next
    return (adjoint_velocity, residual)


def solution(mesh):
    return jax.shard_map(
        local,
        mesh=mesh,
        in_specs=(P(None, None, "gx", "gy"), P(None, "gx", "gy"), P("gx", "gy"), P("gx", "gy")),
        out_specs=(P(None, None, "gx", "gy"), P(None, None, "gx", "gy")),
        check_vma=False,
    )
```

profile of v0, /device:TPU:1, one launch (start us, length us, event | category | flops | bytes accessed | tf_op | source)
XLA Modules:
  0.0 2009.2 jit_solution(4247419242420712863)
XLA Ops:
  1.5 5.4 collective-permute-start.4
  6.9 8.3 collective-permute-start.5
  20.4 1.9 collective-permute-start
  22.3 2.4 collective-permute-start.1
  28.9 4.6 collective-permute-start.2
  34.4 1.8 collective-permute-done.2
  37.3 3.3 stack.36
  40.6 1.4 multiply_bitcast_fusion.2
  45.3 8.6 all-reduce.49
  53.8 380.2 %all-reduce.48 = (f32[]{:T(128)}, f32[]{:T(128)}) all-reduce(f32[]{:T(128)} %get-tuple-element.72, f32[]{:T(128)} %get-tuple-element.73), channel_id=1, replica_groups=mesh['gx'=192,'gy'=4] {'gx'}, use_global_device_ids=true, to_apply=%region_2.0 | all-reduce | flops 2 | bytes 16 | tf_op jit(solution)/shard_map/psum | solution.py:125
  436.1 6.6 psum.88
  442.7 371.5 %psum.89 = f32[]{:T(128)} all-reduce(f32[]{:T(128)} %psum.88), channel_id=1, replica_groups=mesh['gx'=192,'gy'=4] {'gx'}, use_global_device_ids=true, to_apply=%region_8.9 | all-reduce | flops 1 | bytes 8 | tf_op jit(solution)/shard_map/psum | solution.py:125
  815.7 1.9 collective-permute-start.8
  817.6 2.4 collective-permute-start.9
  820.0 2.6 collective-permute-done.9
  824.1 4.4 collective-permute-start.10
  828.6 1.7 collective-permute-done.10
  831.5 3.3 stack.40
  834.7 1.4 multiply_bitcast_fusion.1
  839.3 9.1 psum.90
  848.3 371.3 %psum.91 = f32[]{:T(128)} all-reduce(f32[]{:T(128)} %psum.90), channel_id=1, replica_groups=mesh['gx'=192,'gy'=4] {'gx'}, use_global_device_ids=true, to_apply=%region_11.12 | all-reduce | flops 1 | bytes 8 | tf_op jit(solution)/shard_map/psum | solution.py:125
  1221.7 7.4 psum.92
  1229.1 372.2 %psum.93 = f32[]{:T(128)} all-reduce(f32[]{:T(128)} %psum.92), channel_id=1, replica_groups=mesh['gx'=192,'gy'=4] {'gx'}, use_global_device_ids=true, to_apply=%region_14.15 | all-reduce | flops 1 | bytes 8 | tf_op jit(solution)/shard_map/psum | solution.py:125
  1602.7 1.9 collective-permute-start.12
  1604.6 2.4 collective-permute-start.13
  1607.1 2.6 collective-permute-done.13
  1611.2 4.2 collective-permute-start.14
  1615.6 1.8 collective-permute-done.14
  1618.5 3.3 stack.44
  1621.8 1.4 multiply_bitcast_fusion
  1626.3 8.5 psum.94
  1634.8 371.6 %psum.95 = f32[]{:T(128)} all-reduce(f32[]{:T(128)} %psum.94), channel_id=1, replica_groups=mesh['gx'=192,'gy'=4] {'gx'}, use_global_device_ids=true, to_apply=%region_17.18 | all-reduce | flops 1 | bytes 8 | tf_op jit(solution)/shard_map/psum | solution.py:125
  (126 shorter events, 29.6 us)
Async XLA Ops:
  1.5 15.4 collective-permute-start.4
  6.9 10.0 collective-permute-start.5
  17.8 7.0 collective-permute-start.6
  19.1 6.4 collective-permute-start.7
  20.4 6.2 collective-permute-start
  22.3 5.0 collective-permute-start.1
  27.6 6.8 collective-permute-start.3
  28.9 7.3 collective-permute-start.2
  37.3 3.3 copy-start.1
  43.6 0.7 copy-start.2
  43.6 0.9 copy-start
  815.7 4.3 collective-permute-start.8
  817.6 5.0 collective-permute-start.9
  822.8 5.8 collective-permute-start.11
  824.1 6.2 collective-permute-start.10
  1602.7 4.3 collective-permute-start.12
  1604.6 5.0 collective-permute-start.13
  1609.9 5.7 collective-permute-start.15
  1611.2 6.2 collective-permute-start.14
where the time goes:
time: 2030 us; the launch traced here: 2010 us
  blocking collectives  1910 us (94%)
  starting transfers between devices  46.4 us (2%)
    psum x10, blocking collectives, global_total(): return lax.psum(lax.psum(value, 'gy'), 'gx')  1910 us
  transfers between devices with their start and end apart: 16, of which 9 were waited for; matrix products, arithmetic and copies ran while one was open for 0% of the time, Pallas kernels for 0%

commit v1 on v0

v1 whole, which is shorter than its diff:
```python
import jax
import jax.numpy as jnp
from jax import lax
from jax.experimental import pallas as pl
from jax.experimental.pallas import tpu as pltpu
from jax.sharding import Mesh, PartitionSpec as P

LEVELS = 11
FIELDS = 3 * LEVELS + 2
SCALE = 16.0
SHIFTS = (8.0, 2.0, 20.0)
F32 = jnp.float32
VMEM = pltpu.VMEM

MASS = {"s": 0.25, "d": 1.0 / 12.0}
SLOPE = {"s": 0.0, "d": 1.0}


def field_list(src_ref, eta_ref, fric_ref, mask_ref):
    fields = [src_ref[c, l] for c in (0, 1) for l in range(LEVELS)]
    fields += [eta_ref[l] for l in range(LEVELS)]
    fields += [fric_ref[...], mask_ref[...].astype(F32)]
    return fields


def pack_kernel(src_ref, eta_ref, fric_ref, mask_ref, low_ref, high_ref, down_ref, up_ref):
    lane = lax.broadcasted_iota(jnp.int32, (8, 128), 1)
    low = jnp.zeros((8, 128), F32)
    high = jnp.zeros((8, 128), F32)
    for f, value in enumerate(field_list(src_ref, eta_ref, fric_ref, mask_ref)):
        place = (lane >= 3 * f) & (lane < 3 * f + 3)
        low = jnp.where(place, pltpu.roll(value, 3 * f, 1) if f else value, low)
        high = jnp.where(place, pltpu.roll(value, (3 * f - 125) % 128, 1), high)
        down_ref[f] = value[0:4]
        up_ref[f] = value[4:8]
    low_ref[...] = low
    high_ref[...] = high
    for f in (FIELDS, FIELDS + 1):
        down_ref[f] = jnp.zeros((4, 128), F32)
        up_ref[f] = jnp.zeros((4, 128), F32)


def ahead(value, axis):
    return pltpu.roll(value, value.shape[axis] - 1, axis)


def behind(value, axis):
    return pltpu.roll(value, 1, axis)


def coefficient(mode, cx, cy, cz):
    x, y, z = mode
    total = cx * SLOPE[x] * MASS[y] * MASS[z]
    total += cy * MASS[x] * SLOPE[y] * MASS[z]
    return total + cz * MASS[x] * MASS[y] * SLOPE[z]


def flat_modes(plane):
    after = ahead(plane, 1)
    s, d = plane + after, after - plane
    s1, d1 = ahead(s, 0), ahead(d, 0)
    return {"ss": s + s1, "ds": s1 - s, "sd": d + d1, "dd": d1 - d}


def flat_back(modes):
    s = modes["ss"] - modes["ds"] + behind(modes["ss"] + modes["ds"], 0)
    d = modes["sd"] - modes["dd"] + behind(modes["sd"] + modes["dd"], 0)
    return s - d + behind(s + d, 1)


def layer(lower, upper, eta):
    modes = []
    for c in (0, 1):
        m = {}
        for xy in ("ss", "ds", "sd", "dd"):
            m[xy + "d"] = upper[c][xy] - lower[c][xy]
            if xy != "ss":
                m[xy + "s"] = upper[c][xy] + lower[c][xy]
        modes.append(m)
    low, high = [], []
    for c in (0, 1):
        weights = (4.0, 1.0, 4.0) if c == 0 else (1.0, 4.0, 4.0)
        own, other = modes[c], modes[1 - c]
        out = {}
        for m, value in own.items():
            out[m] = coefficient(m, *weights) * value
        for z in "sd":
            q = 0.25 * MASS[z]
            double, single = ("ds", "sd") if c == 0 else ("sd", "ds")
            out[double + z] = out[double + z] + (2.0 * q) * other[single + z]
            out[single + z] = out[single + z] + q * other[double + z]
        out = {m: value * eta for m, value in out.items()}
        lo, hi = {}, {}
        for xy in ("ss", "ds", "sd", "dd"):
            d = out[xy + "d"]
            s = out.get(xy + "s")
            lo[xy] = -d if s is None else s - d
            hi[xy] = d if s is None else s + d
        low.append(lo)
        high.append(hi)
    return low, high


def krylov_kernel(
    src_ref, eta_ref, fric_ref, mask_ref, left_ref, right_ref, next_ref, prev_ref,
    out_ref, row_ref, vec, cell, frict, mask,
):
    lane = lax.broadcasted_iota(jnp.int32, (16, 128), 1)
    left = jnp.concatenate([left_ref[...], next_ref[FIELDS + 1], prev_ref[FIELDS + 1]], 0)
    right = jnp.concatenate([right_ref[...], next_ref[FIELDS], prev_ref[FIELDS]], 0)
    fields = field_list(src_ref, eta_ref, fric_ref, mask_ref)

    def plane(f):
        own = jnp.concatenate([fields[f], next_ref[f], prev_ref[f]], 0)
        from_left = pltpu.roll(left, (125 - 3 * f) % 128, 1)
        from_right = pltpu.roll(right, (-3 * f) % 128, 1) if f else right
        zero = jnp.zeros((16, 128), F32)
        side = jnp.where(lane >= 125, from_left, jnp.where(lane < 3, from_right, zero))
        return jnp.concatenate([own, side], 1)

    frict[...] = plane(3 * LEVELS) * (1.0 / SCALE)
    mask_plane = plane(3 * LEVELS + 1)
    mask[...] = mask_plane
    for l in range(LEVELS):
        vec[0, 0, l] = plane(l) * mask_plane
        vec[0, 1, l] = plane(LEVELS + l) * mask_plane
    below = None
    for l in range(LEVELS):
        value = plane(2 * LEVELS + l)
        value = value + ahead(value, 1)
        value = value + ahead(value, 0)
        if below is not None:
            cell[l - 1] = (below + value) * (0.125 / SCALE)
        below = value

    for k in range(3):
        shift = SHIFTS[k] / SCALE

        def finish(l, sums):
            for c in (0, 1):
                value = vec[k, c, l]
                image = flat_back(sums[c])
                if l == 0:
                    image = image + frict[...] * value
                vec[k + 1, c, l] = image * mask[...] - shift * value

        lower = [flat_modes(vec[k, c, 0]) for c in (0, 1)]
        pending = None
        for l in range(LEVELS - 1):
            upper = [flat_modes(vec[k, c, l + 1]) for c in (0, 1)]
            low, high = layer(lower, upper, cell[l])
            if pending is not None:
                low = [{m: low[c][m] + pending[c][m] for m in low[c]} for c in (0, 1)]
            finish(l, low)
            lower, pending = upper, high
        finish(LEVELS - 1, pending)

    pairs = ((0, 0), (0, 1), (0, 2), (1, 1), (1, 2), (2, 2), (1, 3), (2, 3))
    sums = [jnp.zeros((8, 128), F32) for _ in pairs]
    for c in (0, 1):
        for l in range(LEVELS):
            v = [vec[k, c, l, 0:8, 0:128] for k in range(4)]
            for k in range(4):
                out_ref[k, c, l] = v[k]
            sums = [s + v[i] * v[j] for s, (i, j) in zip(sums, pairs)]
    stacked = jnp.concatenate([jnp.sum(s, axis=0, keepdims=True) for s in sums], 0)
    totals = jnp.sum(stacked, axis=1, keepdims=True)
    ids = [lax.broadcasted_iota(jnp.int32, (8, 128), a) for a in (0, 1)]
    spread = jnp.where(ids[0] == ids[1], totals, 0.0)
    row_ref[...] = jnp.sum(spread, axis=0, keepdims=True)


def coordinates(gram):
    def dot(a, b):
        total = None
        for i in range(len(a)):
            for j in range(len(b)):
                term = a[i] * b[j] * gram[min(i, j), max(i, j)]
                total = term if total is None else total + term
        return total

    def added(a, b, factor):
        size = max(len(a), len(b))
        out = []
        for i in range(size):
            if i >= len(b):
                out.append(a[i])
            elif i >= len(a):
                out.append(factor * b[i])
            else:
                out.append(a[i] + factor * b[i])
        return out

    one = jnp.ones_like(gram[0, 0])
    residual, direction, answer = [one], [one], []
    norm = gram[0, 0]
    for k in range(3):
        image = [SHIFTS[i] * direction[i] for i in range(k + 1)] + [SCALE * direction[k]]
        for i in range(1, k + 1):
            image[i] = image[i] + SCALE * direction[i - 1]
        alpha = norm / dot(direction, image)
        answer = added(answer, direction, alpha)
        residual = added(residual, image, -alpha)
        if k < 2:
            fresh = dot(residual, residual)
            direction = added(residual, direction, fresh / norm)
            norm = fresh
    return answer, residual


def combine_kernel(vec_ref, rows_ref, answer_ref, residual_ref):
    row = jnp.sum(rows_ref[...], axis=0, keepdims=True)
    ids = [lax.broadcasted_iota(jnp.int32, (8, 128), a) for a in (0, 1)]
    totals = jnp.sum(jnp.where(ids[0] == ids[1], row, 0.0), axis=1, keepdims=True)
    tile = jnp.broadcast_to(totals, (8, 128))
    pairs = ((0, 0), (0, 1), (0, 2), (1, 1), (1, 2), (2, 2), (1, 3), (2, 3))
    gram = {pair: tile[n : n + 1] for n, pair in enumerate(pairs)}
    gram[0, 3] = gram[1, 2] + ((SHIFTS[0] - SHIFTS[2]) / SCALE) * gram[0, 2]
    answer, residual = coordinates(gram)
    answer = [jnp.broadcast_to(a, (8, 128)) for a in answer]
    residual = [jnp.broadcast_to(a, (8, 128)) for a in residual]
    for c in (0, 1):
        for l in range(LEVELS):
            v = [vec_ref[k, c, l] for k in range(4)]
            answer_ref[c, l] = answer[0] * v[0] + answer[1] * v[1] + answer[2] * v[2]
            residual_ref[c, l] = (
                residual[0] * v[0] + residual[1] * v[1] + residual[2] * v[2] + residual[3] * v[3]
            )


def vmem(n):
    return [pl.BlockSpec(memory_space=VMEM)] * n


def shape(*dims):
    return jax.ShapeDtypeStruct(dims, F32)


def everywhere(row, axes):
    size = lax.axis_size(axes)
    spread = jnp.broadcast_to(row[None], (size, 1, 128))
    return lax.all_to_all(spread, axes, 0, 0, tiled=True)


def local(adjoint_source, viscosity, friction, ice_mask):
    gx, gy = ("far", "near"), "gy"
    size_x, size_y = lax.axis_size(gx), lax.axis_size(gy)
    fields = (adjoint_source, viscosity, friction, ice_mask)
    low, high, down, up = pl.pallas_call(
        pack_kernel,
        out_shape=(shape(8, 128), shape(8, 128), shape(FIELDS + 2, 4, 128), shape(FIELDS + 2, 4, 128)),
        in_specs=vmem(4),
        out_specs=tuple(vmem(4)),
    )(*fields)
    right = lax.ppermute(low, gy, [(i + 1, i) for i in range(size_y - 1)])
    left = lax.ppermute(high, gy, [(i, i + 1) for i in range(size_y - 1)])
    down = down.at[FIELDS:].set(jnp.stack([right[0:4], left[0:4]]))
    up = up.at[FIELDS:].set(jnp.stack([right[4:8], left[4:8]]))
    following = lax.ppermute(down, gx, [(i + 1, i) for i in range(size_x - 1)])
    previous = lax.ppermute(up, gx, [(i, i + 1) for i in range(size_x - 1)])
    vectors, row = pl.pallas_call(
        krylov_kernel,
        out_shape=(shape(4, 2, LEVELS, 8, 128), shape(1, 128)),
        in_specs=vmem(8),
        out_specs=tuple(vmem(2)),
        scratch_shapes=[
            VMEM((4, 2, LEVELS, 16, 256), F32),
            VMEM((LEVELS - 1, 16, 256), F32),
            VMEM((16, 256), F32),
            VMEM((16, 256), F32),
        ],
    )(*fields, left, right, following, previous)
    row = jnp.sum(everywhere(row, "near"), axis=0)
    rows = everywhere(row, ("far", "gy"))[:, 0]
    return pl.pallas_call(
        combine_kernel,
        out_shape=(shape(2, LEVELS, 8, 128), shape(2, LEVELS, 8, 128)),
        in_specs=vmem(2),
        out_specs=tuple(vmem(2)),
    )(vectors, rows)


def solution(mesh):
    size_x, size_y = mesh.devices.shape
    split = Mesh(mesh.devices.reshape(8, size_x // 8, size_y), ("far", "near", "gy"))
    gx = ("far", "near")
    vector, plane = P(None, None, gx, "gy"), P(gx, "gy")
    return jax.shard_map(
        local,
        mesh=split,
        in_specs=(vector, P(None, gx, "gy"), plane, plane),
        out_specs=(vector, vector),
        check_vma=False,
    )
```

time: 2030 us -> 76.8 us (0.04); the launches traced: 2010 us -> 76.4 us
  blocking collectives: 1910 us -> 41.1 us
  starting transfers between devices: 46.4 us -> 17.4 us
    psum x10 -> x0, blocking collectives: 1910 us -> none  [global_total(): return lax.psum(lax.psum(value, 'gy'), 'gx')]
    all_to_all x0 -> x2, blocking collectives: none -> 41.1 us  [everywhere(): return lax.all_to_all(spread, axes, 0, 0, tiled=True)]
    ppermute x16 -> x4, starting transfers between devices: 46.4 us -> 17.4 us  [the longest x1 6.21 us: local(): following = lax.ppermute(down, gx, [(i + 1, i) for i in range(size_x - 1)])]
  transfers between devices with their start and end apart: 16 -> 4, of which waited for: 9 -> 2; matrix products, arithmetic and copies ran while one was open for 0% -> 1% of each run, Pallas kernels for 0% -> 0%
where the time goes in v1:
time: 76.8 us; the launch traced here: 76.4 us
  blocking collectives  41.1 us (54%)
  starting transfers between devices  17.4 us (23%)
  Pallas kernels  9.76 us (13%)
  waiting for transfers between devices  3.75 us (5%)
  local copies, waits for them, and re-layouts  2.45 us (3%)
  other arithmetic  1.21 us (2%)
    all_to_all x2, blocking collectives, everywhere(): return lax.all_to_all(spread, axes, 0, 0, tiled=True)  41.1 us
    ppermute x1, starting transfers between devices, local(): following = lax.ppermute(down, gx, [(i + 1, i) for i in range(size_x - 1)])  6.21 us
    pallas_call x1, Pallas kernels, local(): pl.pallas_call(krylov_kernel, out_shape=(shape(4, 2, LEVELS, 8, 128), sha...  6.2 us
    ppermute x1, starting transfers between devices, local(): previous = lax.ppermute(up, gx, [(i, i + 1) for i in range(size_x - 1)])  5.98 us
    ppermute x1, starting transfers between devices, local(): left = lax.ppermute(high, gy, [(i, i + 1) for i in range(size_y - 1)])  3.93 us
    ppermute x1, waiting for transfers between devices, local(): right = lax.ppermute(low, gy, [(i + 1, i) for i in range(size_y - 1)])  2.67 us
    unnamed x10, local copies, waits for them, and re-layouts  2.42 us
    pallas_call x1, Pallas kernels, local(): pl.pallas_call(combine_kernel, out_shape=(shape(2, LEVELS, 8, 128), shape...  1.86 us
  transfers between devices with their start and end apart: 4, of which 2 were waited for; matrix products, arithmetic and copies ran while one was open for 1% of the time, Pallas kernels for 0%

profile of v1, /device:TPU:1, one launch (start us, length us, event | category | flops | bytes accessed | tf_op | source)
XLA Modules:
  0.0 76.4 jit_solution(7536389238934837730)
XLA Ops:
  0.6 1.7 %shard_map.59 = (f32[8,128]{1,0:T(8,128)}, f32[8,128]{1,0:T(8,128)}, f32[37,4,128]{2,1,0:T(4,128)}, f32[37,4,128]{2,1,0:T(4,128)}) custom-call(f32[2,11,8,128]{3,2,1,0:T(8,128)} %src_ref.3, f32[11,8,128]{2,1,0:T(8,128)} %eta_ref.3, f32[8,128]{1,0:T(8,128)} %fric_ref.3, s32[8,128]{1,0:T(8,128)} %mask_ref.3), custom_call_target="tpu_custom_call" | custom-call | tf_op jit(solution)/shard_map/pallas_call | solution.py:249
  2.3 3.9 %collective-permute-start = (f32[8,128]{1,0:T(8,128)}, f32[8,128]{1,0:T(8,128)S(1)}, u32[]{:S(2)}, u32[]{:S(2)}) collective-permute-start(f32[8,128]{1,0:T(8,128)} %get-tuple-element.32), channel_id=1, source_target_pairs={{0,1},{1,2},{2,3},{4,5},{5,6},{6,7},{8,9},{9,10},{10,11},{12,13},{... | collective-permute-start | bytes 12296 | tf_op jit(solution)/shard_map/ppermute | solution.py:256
  6.3 1.3 %collective-permute-start.1 = (f32[8,128]{1,0:T(8,128)}, f32[8,128]{1,0:T(8,128)S(1)}, u32[]{:S(2)}, u32[]{:S(2)}) collective-permute-start(f32[8,128]{1,0:T(8,128)} %get-tuple-element.33), channel_id=1, source_target_pairs={{1,0},{2,1},{3,2},{5,4},{6,5},{7,6},{9,8},{10,9},{11,10},{13,12},{... | collective-permute-start | bytes 12296 | tf_op jit(solution)/shard_map/ppermute | solution.py:255
  7.6 0.0 collective-permute-done.left_ref
  7.6 0.0 copy-start.2
  7.6 0.6 copy-done.2
  8.2 2.7 %collective-permute-done.1.right_ref = f32[8,128]{1,0:T(8,128)S(1)} collective-permute-done((f32[8,128]{1,0:T(8,128)}, f32[8,128]{1,0:T(8,128)S(1)}, u32[]{:S(2)}, u32[]{:S(2)}) %collective-permute-start.1) | collective-permute-done | bytes 4128 | tf_op jit(solution)/shard_map/ppermute | solution.py:255
  10.8 0.0 copy-start.3
  10.8 0.6 copy-done.3
  11.4 0.6 maximum_dynamic-update-slice_fusion.1
  12.0 6.0 %collective-permute-start.3 = (f32[37,4,128]{2,1,0:T(4,128)}, f32[37,4,128]{2,1,0:T(4,128)S(1)}, u32[]{:S(2)}, u32[]{:S(2)}) collective-permute-start(f32[37,4,128]{2,1,0:T(4,128)} %maximum_dynamic-update-slice_fusion.1), channel_id=1, source_target_pairs={{0,4},{4,8},{8,12},{12,16},{16,20},{20,24},{24,28},{28,32},{32,36}... | collective-permute-start | bytes 227336 | tf_op jit(solution)/shard_map/ppermute | solution.py:260
  18.0 0.6 maximum_dynamic-update-slice_fusion
  18.6 6.2 %collective-permute-start.2 = (f32[37,4,128]{2,1,0:T(4,128)}, f32[37,4,128]{2,1,0:T(4,128)S(1)}, u32[]{:S(2)}, u32[]{:S(2)}) collective-permute-start(f32[37,4,128]{2,1,0:T(4,128)} %maximum_dynamic-update-slice_fusion), channel_id=1, source_target_pairs={{4,0},{8,4},{12,8},{16,12},{20,16},{24,20},{28,24},{32,28},{36,32}... | collective-permute-start | bytes 227336 | tf_op jit(solution)/shard_map/ppermute | solution.py:259
  24.8 0.0 collective-permute-done.3.prev_ref
  24.8 0.0 copy-start
  24.9 1.1 %collective-permute-done.2.next_ref = f32[37,4,128]{2,1,0:T(4,128)S(1)} collective-permute-done((f32[37,4,128]{2,1,0:T(4,128)}, f32[37,4,128]{2,1,0:T(4,128)S(1)}, u32[]{:S(2)}, u32[]{:S(2)}) %collective-permute-start.2) | collective-permute-done | bytes 75808 | tf_op jit(solution)/shard_map/ppermute | solution.py:259
  25.9 0.0 copy-done
  25.9 0.0 copy-start.1
  25.9 0.6 copy-done.1
  26.6 6.2 %shard_map.60 = (f32[4,2,11,8,128]{4,3,2,1,0:T(8,128)}, f32[1,128]{1,0:T(1,128)}) custom-call(f32[2,11,8,128]{3,2,1,0:T(8,128)} %src_ref.3, f32[11,8,128]{2,1,0:T(8,128)} %eta_ref.3, f32[8,128]{1,0:T(8,128)} %fric_ref.3, s32[8,128]{1,0:T(8,128)} %mask_ref.3, f32[8,128]{1,0:T(8,128)} %copy-done.2, f32[8,128]{1,0:T(8,128)} %copy-done.3, ...), custom_call_target="tpu_custom_call" | custom-call | tf_op jit(solution)/shard_map/pallas_call | solution.py:261
  32.8 0.0 copy-start.4
  32.8 0.6 copy-done.4
  33.4 23.4 %all_to_all.10 = f32[24,1,128]{2,1,0:T(1,128)S(1)} all-to-all(f32[24,1,128]{2,1,0:T(1,128)S(1)} %broadcast_in_dim.7), channel_id=1, replica_groups=mesh['far'=8,'near'=24,'gy'=4] {'near'}, dimensions={0} | all-to-all | bytes 24576 | tf_op jit(solution)/shard_map/all_to_all | solution.py:242
  56.8 17.7 %all_to_all.11 = f32[32,1,128]{2,1,0:T(1,128)} all-to-all(f32[32,1,128]{2,1,0:T(1,128)S(1)} %broadcast_in_dim.16), channel_id=1, replica_groups=mesh['far'=8,'near'=24,'gy'=4] {'far','gy'}, dimensions={0} | all-to-all | bytes 32768 | tf_op jit(solution)/shard_map/all_to_all | solution.py:242
  74.6 1.9 %shard_map.61 = (f32[2,11,8,128]{3,2,1,0:T(8,128)}, f32[2,11,8,128]{3,2,1,0:T(8,128)}) custom-call(f32[4,2,11,8,128]{4,3,2,1,0:T(8,128)} %get-tuple-element.36.vec_ref, f32[32,128]{1,0:T(8,128)} %bitcast.11), custom_call_target="tpu_custom_call" | custom-call | tf_op jit(solution)/shard_map/pallas_call | solution.py:275
  (5 shorter events, 0.0 us)
Async XLA Ops:
  2.3 5.2 %collective-permute-start = (f32[8,128]{1,0:T(8,128)}, f32[8,128]{1,0:T(8,128)S(1)}, u32[]{:S(2)}, u32[]{:S(2)}) collective-permute-start(f32[8,128]{1,0:T(8,128)} %get-tuple-element.32), channel_id=1, source_target_pairs={{0,1},{1,2},{2,3},{4,5},{5,6},{6,7},{8,9},{9,10},{10,11},{12,13},{... | collective-permute-start | bytes 12296 | tf_op jit(solution)/shard_map/ppermute | solution.py:256
  6.3 4.6 %collective-permute-start.1 = (f32[8,128]{1,0:T(8,128)}, f32[8,128]{1,0:T(8,128)S(1)}, u32[]{:S(2)}, u32[]{:S(2)}) collective-permute-start(f32[8,128]{1,0:T(8,128)} %get-tuple-element.33), channel_id=1, source_target_pairs={{1,0},{2,1},{3,2},{5,4},{6,5},{7,6},{9,8},{10,9},{11,10},{13,12},{... | collective-permute-start | bytes 12296 | tf_op jit(solution)/shard_map/ppermute | solution.py:255
  7.6 0.6 copy-start.2
  10.8 0.6 copy-start.3
  12.0 12.8 %collective-permute-start.3 = (f32[37,4,128]{2,1,0:T(4,128)}, f32[37,4,128]{2,1,0:T(4,128)S(1)}, u32[]{:S(2)}, u32[]{:S(2)}) collective-permute-start(f32[37,4,128]{2,1,0:T(4,128)} %maximum_dynamic-update-slice_fusion.1), channel_id=1, source_target_pairs={{0,4},{4,8},{8,12},{12,16},{16,20},{20,24},{24,28},{28,32},{32,36}... | collective-permute-start | bytes 227336 | tf_op jit(solution)/shard_map/ppermute | solution.py:260
  18.6 7.3 %collective-permute-start.2 = (f32[37,4,128]{2,1,0:T(4,128)}, f32[37,4,128]{2,1,0:T(4,128)S(1)}, u32[]{:S(2)}, u32[]{:S(2)}) collective-permute-start(f32[37,4,128]{2,1,0:T(4,128)} %maximum_dynamic-update-slice_fusion), channel_id=1, source_target_pairs={{4,0},{8,4},{12,8},{16,12},{20,16},{24,20},{28,24},{32,28},{36,32}... | collective-permute-start | bytes 227336 | tf_op jit(solution)/shard_map/ppermute | solution.py:259
  24.8 1.1 %copy-start = (f32[37,4,128]{2,1,0:T(4,128)}, f32[37,4,128]{2,1,0:T(4,128)S(1)}, u32[]{:S(2)}) copy-start(f32[37,4,128]{2,1,0:T(4,128)S(1)} %collective-permute-done.3.prev_ref) | copy-start | bytes 227332
  25.9 0.6 copy-start.1
  32.8 0.6 copy-start.4

commit v2 on v1

--- a/solution.py
+++ b/solution.py
@@ -16,28 +16,40 @@
 SLOPE = {"s": 0.0, "d": 1.0}
 
 
-def field_list(src_ref, eta_ref, fric_ref, mask_ref):
-    fields = [src_ref[c, l] for c in (0, 1) for l in range(LEVELS)]
-    fields += [eta_ref[l] for l in range(LEVELS)]
-    fields += [fric_ref[...], mask_ref[...].astype(F32)]
-    return fields
-
-
-def pack_kernel(src_ref, eta_ref, fric_ref, mask_ref, low_ref, high_ref, down_ref, up_ref):
+def side_kernel(src_ref, eta_ref, fric_ref, mask_ref, fields_ref, low_ref, high_ref, mask, sems):
+    parts = [
+        (src_ref.at[0], fields_ref.at[0:LEVELS]),
+        (src_ref.at[1], fields_ref.at[LEVELS : 2 * LEVELS]),
+        (eta_ref, fields_ref.at[2 * LEVELS : 3 * LEVELS]),
+        (fric_ref, fields_ref.at[3 * LEVELS]),
+        (mask_ref, mask),
+    ]
+    copies = [pltpu.make_async_copy(a, b, sems.at[n]) for n, (a, b) in enumerate(parts)]
+    for copy in copies:
+        copy.start()
+    for copy in copies:
+        copy.wait()
+    fields_ref[FIELDS - 1] = mask[...].astype(F32)
     lane = lax.broadcasted_iota(jnp.int32, (8, 128), 1)
     low = jnp.zeros((8, 128), F32)
     high = jnp.zeros((8, 128), F32)
-    for f, value in enumerate(field_list(src_ref, eta_ref, fric_ref, mask_ref)):
+    for f in range(FIELDS):
+        value = fields_ref[f]
         place = (lane >= 3 * f) & (lane < 3 * f + 3)
         low = jnp.where(place, pltpu.roll(value, 3 * f, 1) if f else value, low)
         high = jnp.where(place, pltpu.roll(value, (3 * f - 125) % 128, 1), high)
+    low_ref[...] = low
+    high_ref[...] = high
+
+
+def rows_kernel(fields_ref, right_ref, left_ref, down_ref, up_ref):
+    for f in range(FIELDS):
+        value = fields_ref[f]
         down_ref[f] = value[0:4]
         up_ref[f] = value[4:8]
-    low_ref[...] = low
-    high_ref[...] = high
-    for f in (FIELDS, FIELDS + 1):
-        down_ref[f] = jnp.zeros((4, 128), F32)
-        up_ref[f] = jnp.zeros((4, 128), F32)
+    for f, value in ((FIELDS, right_ref[...]), (FIELDS + 1, left_ref[...])):
+        down_ref[f] = value[0:4]
+        up_ref[f] = value[4:8]
 
 
 def ahead(value, axis):
@@ -102,16 +114,14 @@
 
 
 def krylov_kernel(
-    src_ref, eta_ref, fric_ref, mask_ref, left_ref, right_ref, next_ref, prev_ref,
+    fields_ref, left_ref, right_ref, next_ref, prev_ref,
     out_ref, row_ref, vec, cell, frict, mask,
 ):
     lane = lax.broadcasted_iota(jnp.int32, (16, 128), 1)
     left = jnp.concatenate([left_ref[...], next_ref[FIELDS + 1], prev_ref[FIELDS + 1]], 0)
     right = jnp.concatenate([right_ref[...], next_ref[FIELDS], prev_ref[FIELDS]], 0)
-    fields = field_list(src_ref, eta_ref, fric_ref, mask_ref)
-
     def plane(f):
-        own = jnp.concatenate([fields[f], next_ref[f], prev_ref[f]], 0)
+        own = jnp.concatenate([fields_ref[f], next_ref[f], prev_ref[f]], 0)
         from_left = pltpu.roll(left, (125 - 3 * f) % 128, 1)
         from_right = pltpu.roll(right, (-3 * f) % 128, 1) if f else right
         zero = jnp.zeros((16, 128), F32)
@@ -228,8 +238,18 @@
             )
 
 
-def vmem(n):
-    return [pl.BlockSpec(memory_space=VMEM)] * n
+def call(kernel, outs, megabytes, *scratch, space=VMEM):
+    def run(*args):
+        return pl.pallas_call(
+            kernel,
+            out_shape=tuple(outs),
+            in_specs=[pl.BlockSpec(memory_space=space)] * len(args),
+            out_specs=tuple([pl.BlockSpec(memory_space=VMEM)] * len(outs)),
+            scratch_shapes=list(scratch),
+            compiler_params=pltpu.CompilerParams(vmem_limit_bytes=megabytes << 20),
+        )(*args)
+
+    return run
 
 
 def shape(*dims):
@@ -242,42 +262,34 @@
     return lax.all_to_all(spread, axes, 0, 0, tiled=True)
 
 
-def local(adjoint_source, viscosity, friction, ice_mask):
+def local(*arguments):
     gx, gy = ("far", "near"), "gy"
     size_x, size_y = lax.axis_size(gx), lax.axis_size(gy)
-    fields = (adjoint_source, viscosity, friction, ice_mask)
-    low, high, down, up = pl.pallas_call(
-        pack_kernel,
-        out_shape=(shape(8, 128), shape(8, 128), shape(FIELDS + 2, 4, 128), shape(FIELDS + 2, 4, 128)),
-        in_specs=vmem(4),
-        out_specs=tuple(vmem(4)),
-    )(*fields)
+    fields, low, high = call(
+        side_kernel,
+        [shape(FIELDS, 8, 128), shape(8, 128), shape(8, 128)],
+        2,
+        VMEM((8, 128), jnp.int32),
+        pltpu.SemaphoreType.DMA((5,)),
+        space=pltpu.HBM,
+    )(*[pltpu.with_memory_space_constraint(a, pltpu.HBM) for a in arguments])
+    left = lax.ppermute(high, gy, [(i, i + 1) for i in range(size_y - 1)])
     right = lax.ppermute(low, gy, [(i + 1, i) for i in range(size_y - 1)])
-    left = lax.ppermute(high, gy, [(i, i + 1) for i in range(size_y - 1)])
-    down = down.at[FIELDS:].set(jnp.stack([right[0:4], left[0:4]]))
-    up = up.at[FIELDS:].set(jnp.stack([right[4:8], left[4:8]]))
+    down, up = call(rows_kernel, [shape(FIELDS + 2, 4, 128)] * 2, 2)(fields, right, left)
     following = lax.ppermute(down, gx, [(i + 1, i) for i in range(size_x - 1)])
     previous = lax.ppermute(up, gx, [(i, i + 1) for i in range(size_x - 1)])
-    vectors, row = pl.pallas_call(
+    vectors, row = call(
         krylov_kernel,
-        out_shape=(shape(4, 2, LEVELS, 8, 128), shape(1, 128)),
-        in_specs=vmem(8),
-        out_specs=tuple(vmem(2)),
-        scratch_shapes=[
-            VMEM((4, 2, LEVELS, 16, 256), F32),
-            VMEM((LEVELS - 1, 16, 256), F32),
-            VMEM((16, 256), F32),
-            VMEM((16, 256), F32),
-        ],
-    )(*fields, left, right, following, previous)
+        [shape(4, 2, LEVELS, 8, 128), shape(1, 128)],
+        8,
+        VMEM((4, 2, LEVELS, 16, 256), F32),
+        VMEM((LEVELS - 1, 16, 256), F32),
+        VMEM((16, 256), F32),
+        VMEM((16, 256), F32),
+    )(fields, left, right, following, previous)
     row = jnp.sum(everywhere(row, "near"), axis=0)
     rows = everywhere(row, ("far", "gy"))[:, 0]
-    return pl.pallas_call(
-        combine_kernel,
-        out_shape=(shape(2, LEVELS, 8, 128), shape(2, LEVELS, 8, 128)),
-        in_specs=vmem(2),
-        out_specs=tuple(vmem(2)),
-    )(vectors, rows)
+    return call(combine_kernel, [shape(2, LEVELS, 8, 128)] * 2, 4)(vectors, rows)
 
 
 def solution(mesh):

time: 76.8 us -> 69.3 us (0.902)
  Pallas kernels: 9.76 us -> 6.43 us
  local copies, waits for them, and re-layouts: 2.45 us -> 0.02 us
  blocking collectives: 41.1 us -> 39.3 us
  other arithmetic: 1.21 us -> 0.02 us
    ppermute x1, starting transfers between devices: 6.21 us -> 10.9 us  [local(): following = lax.ppermute(down, gx, [(i + 1, i) for i in range(size_x - 1)])]
    ppermute x1, starting transfers between devices: 5.98 us -> 1.92 us  [local(): previous = lax.ppermute(up, gx, [(i, i + 1) for i in range(size_x - 1)])]
    pallas_call x3 -> x4, Pallas kernels: 9.76 us -> 6.43 us  [run(): pl.pallas_call(kernel, out_shape=tuple(outs), in_specs=[pl.BlockSpec(memo...]
    unnamed x10 -> x0, local copies, waits for them, and re-layouts: 2.42 us -> none
    all_to_all x2, blocking collectives: 41.1 us -> 39.3 us  [everywhere(): return lax.all_to_all(spread, axes, 0, 0, tiled=True)]
    ppermute x1, waiting for transfers between devices: 0.01 us -> 1.4 us  [local(): previous = lax.ppermute(up, gx, [(i, i + 1) for i in range(size_x - 1)])]
    scatter x2 -> x0, other arithmetic: 1.2 us -> none  [the longest x1 0.6 us: local(): down = down.at[FIELDS:].set(jnp.stack([right[0:4], left[0:4]]))]
    ppermute x1, waiting for transfers between devices: 1.08 us -> 0.01 us  [local(): following = lax.ppermute(down, gx, [(i + 1, i) for i in range(size_x - 1)])]
  transfers between devices with their start and end apart: 4 -> 4, of which waited for: 2 -> 2; matrix products, arithmetic and copies ran while one was open for 1% -> 0% of each run, Pallas kernels for 0% -> 0%
where the time goes in v2:
time: 69.3 us; the launch traced here: 69 us
  blocking collectives  39.3 us (57%)
  starting transfers between devices  18.1 us (26%)
  Pallas kernels  6.43 us (9%)
  waiting for transfers between devices  4.44 us (6%)
  between operations  0.7 us (1%)
    all_to_all x2, blocking collectives, everywhere(): return lax.all_to_all(spread, axes, 0, 0, tiled=True)  39.3 us
    ppermute x1, starting transfers between devices, local(): following = lax.ppermute(down, gx, [(i + 1, i) for i in range(size_x - 1)])  10.9 us
    pallas_call x4, Pallas kernels, run(): pl.pallas_call(kernel, out_shape=tuple(outs), in_specs=[pl.BlockSpec(memo...  6.43 us
    ppermute x1, starting transfers between devices, local(): left = lax.ppermute(high, gy, [(i, i + 1) for i in range(size_y - 1)])  3.94 us
    ppermute x1, waiting for transfers between devices, local(): right = lax.ppermute(low, gy, [(i + 1, i) for i in range(size_y - 1)])  3.04 us
    ppermute x1, starting transfers between devices, local(): previous = lax.ppermute(up, gx, [(i, i + 1) for i in range(size_x - 1)])  1.92 us
    ppermute x1, waiting for transfers between devices, local(): previous = lax.ppermute(up, gx, [(i, i + 1) for i in range(size_x - 1)])  1.4 us
  transfers between devices with their start and end apart: 4, of which 2 were waited for; matrix products, arithmetic and copies ran while one was open for 0% of the time, Pallas kernels for 0%

profile of v2, /device:TPU:1, one launch (start us, length us, event | category | flops | bytes accessed | tf_op | source)
XLA Modules:
  0.0 69.0 jit_solution(9168566601772584320)
XLA Ops:
  0.6 1.0 %shard_map.59 = (f32[35,8,128]{2,1,0:T(8,128)S(1)}, f32[8,128]{1,0:T(8,128)S(1)}, f32[8,128]{1,0:T(8,128)S(1)}) custom-call(f32[2,11,8,128]{3,2,1,0:T(8,128)} %src_ref.1, f32[11,8,128]{2,1,0:T(8,128)} %eta_ref.1, f32[8,128]{1,0:T(8,128)} %fric_ref.1, s32[8,128]{1,0:T(8,128)} %mask_ref.1), custom_call_target="tpu_custom_call" | custom-call | tf_op jit(solution)/shard_map/pallas_call | solution.py:243
  1.7 3.9 %collective-permute-start = (f32[8,128]{1,0:T(8,128)S(1)}, f32[8,128]{1,0:T(8,128)S(1)}, u32[]{:S(2)}, u32[]{:S(2)}) collective-permute-start(f32[8,128]{1,0:T(8,128)S(1)} %get-tuple-element.10), channel_id=1, source_target_pairs={{0,1},{1,2},{2,3},{4,5},{5,6},{6,7},{8,9},{9,10},{10,11},{12,13},{... | collective-permute-start | bytes 12296 | tf_op jit(solution)/shard_map/ppermute | solution.py:276
  5.6 1.3 %collective-permute-start.1 = (f32[8,128]{1,0:T(8,128)S(1)}, f32[8,128]{1,0:T(8,128)S(1)}, u32[]{:S(2)}, u32[]{:S(2)}) collective-permute-start(f32[8,128]{1,0:T(8,128)S(1)} %get-tuple-element.11), channel_id=1, source_target_pairs={{1,0},{2,1},{3,2},{5,4},{6,5},{7,6},{9,8},{10,9},{11,10},{13,12},{... | collective-permute-start | bytes 12296 | tf_op jit(solution)/shard_map/ppermute | solution.py:277
  6.9 0.0 collective-permute-done.left_ref
  6.9 3.0 %collective-permute-done.1.right_ref = f32[8,128]{1,0:T(8,128)S(1)} collective-permute-done((f32[8,128]{1,0:T(8,128)S(1)}, f32[8,128]{1,0:T(8,128)S(1)}, u32[]{:S(2)}, u32[]{:S(2)}) %collective-permute-start.1) | collective-permute-done | bytes 4128 | tf_op jit(solution)/shard_map/ppermute | solution.py:277
  10.0 10.9 %collective-permute-start.2 = (f32[37,4,128]{2,1,0:T(4,128)S(1)}, f32[37,4,128]{2,1,0:T(4,128)S(1)}, u32[]{:S(2)}, u32[]{:S(2)}) collective-permute-start(f32[37,4,128]{2,1,0:T(4,128)S(1)} %get-tuple-element.12), channel_id=1, source_target_pairs={{4,0},{8,4},{12,8},{16,12},{20,16},{24,20},{28,24},{32,28},{36,32}... | collective-permute-start | bytes 227336 | tf_op jit(solution)/shard_map/ppermute | solution.py:279
  20.9 1.9 %collective-permute-start.3 = (f32[37,4,128]{2,1,0:T(4,128)S(1)}, f32[37,4,128]{2,1,0:T(4,128)S(1)}, u32[]{:S(2)}, u32[]{:S(2)}) collective-permute-start(f32[37,4,128]{2,1,0:T(4,128)S(1)} %get-tuple-element.13), channel_id=1, source_target_pairs={{0,4},{4,8},{8,12},{12,16},{16,20},{20,24},{24,28},{28,32},{32,36}... | collective-permute-start | bytes 227336 | tf_op jit(solution)/shard_map/ppermute | solution.py:280
  22.8 0.0 collective-permute-done.2.next_ref
  22.9 1.4 %collective-permute-done.3.prev_ref = f32[37,4,128]{2,1,0:T(4,128)S(1)} collective-permute-done((f32[37,4,128]{2,1,0:T(4,128)S(1)}, f32[37,4,128]{2,1,0:T(4,128)S(1)}, u32[]{:S(2)}, u32[]{:S(2)}) %collective-permute-start.3) | collective-permute-done | bytes 75808 | tf_op jit(solution)/shard_map/ppermute | solution.py:280
  24.2 4.5 %shard_map.61 = (f32[4,2,11,8,128]{4,3,2,1,0:T(8,128)S(1)}, f32[1,128]{1,0:T(1,128)S(1)}) custom-call(f32[35,8,128]{2,1,0:T(8,128)S(1)} %get-tuple-element.9.fields_ref, f32[8,128]{1,0:T(8,128)S(1)} %collective-permute-done.left_ref, f32[8,128]{1,0:T(8,128)S(1)} %collective-permute-done.1.right_ref, f32[37,4,128]{2,1,0:T(4,128)S(1)} %collective-permute-done.2.next_ref, ...), custom_call_target="tpu_custom_call" | custom-call | tf_op jit(solution)/shard_map/pallas_call | solution.py:243
  28.8 19.9 %all_to_all.10 = f32[24,1,128]{2,1,0:T(1,128)S(1)} all-to-all(f32[24,1,128]{2,1,0:T(1,128)S(1)} %broadcast_in_dim.7), channel_id=1, replica_groups=mesh['far'=8,'near'=24,'gy'=4] {'near'}, dimensions={0} | all-to-all | bytes 24576 | tf_op jit(solution)/shard_map/all_to_all | solution.py:262
  48.7 19.4 %all_to_all.11 = f32[32,1,128]{2,1,0:T(1,128)S(1)} all-to-all(f32[32,1,128]{2,1,0:T(1,128)S(1)} %broadcast_in_dim.16), channel_id=1, replica_groups=mesh['far'=8,'near'=24,'gy'=4] {'far','gy'}, dimensions={0} | all-to-all | bytes 32768 | tf_op jit(solution)/shard_map/all_to_all | solution.py:262
  68.1 0.9 %shard_map.62 = (f32[2,11,8,128]{3,2,1,0:T(8,128)}, f32[2,11,8,128]{3,2,1,0:T(8,128)}) custom-call(f32[4,2,11,8,128]{4,3,2,1,0:T(8,128)S(1)} %get-tuple-element.14.vec_ref, f32[32,128]{1,0:T(8,128)S(1)} %bitcast.3), custom_call_target="tpu_custom_call" | custom-call | tf_op jit(solution)/shard_map/pallas_call | solution.py:243
  (4 shorter events, 0.1 us)
Async XLA Ops:
  1.7 5.3 %collective-permute-start = (f32[8,128]{1,0:T(8,128)S(1)}, f32[8,128]{1,0:T(8,128)S(1)}, u32[]{:S(2)}, u32[]{:S(2)}) collective-permute-start(f32[8,128]{1,0:T(8,128)S(1)} %get-tuple-element.10), channel_id=1, source_target_pairs={{0,1},{1,2},{2,3},{4,5},{5,6},{6,7},{8,9},{9,10},{10,11},{12,13},{... | collective-permute-start | bytes 12296 | tf_op jit(solution)/shard_map/ppermute | solution.py:276
  5.6 4.4 %collective-permute-start.1 = (f32[8,128]{1,0:T(8,128)S(1)}, f32[8,128]{1,0:T(8,128)S(1)}, u32[]{:S(2)}, u32[]{:S(2)}) collective-permute-start(f32[8,128]{1,0:T(8,128)S(1)} %get-tuple-element.11), channel_id=1, source_target_pairs={{1,0},{2,1},{3,2},{5,4},{6,5},{7,6},{9,8},{10,9},{11,10},{13,12},{... | collective-permute-start | bytes 12296 | tf_op jit(solution)/shard_map/ppermute | solution.py:277
  10.0 12.9 %collective-permute-start.2 = (f32[37,4,128]{2,1,0:T(4,128)S(1)}, f32[37,4,128]{2,1,0:T(4,128)S(1)}, u32[]{:S(2)}, u32[]{:S(2)}) collective-permute-start(f32[37,4,128]{2,1,0:T(4,128)S(1)} %get-tuple-element.12), channel_id=1, source_target_pairs={{4,0},{8,4},{12,8},{16,12},{20,16},{24,20},{28,24},{32,28},{36,32}... | collective-permute-start | bytes 227336 | tf_op jit(solution)/shard_map/ppermute | solution.py:279
  20.9 3.3 %collective-permute-start.3 = (f32[37,4,128]{2,1,0:T(4,128)S(1)}, f32[37,4,128]{2,1,0:T(4,128)S(1)}, u32[]{:S(2)}, u32[]{:S(2)}) collective-permute-start(f32[37,4,128]{2,1,0:T(4,128)S(1)} %get-tuple-element.13), channel_id=1, source_target_pairs={{0,4},{4,8},{8,12},{12,16},{16,20},{20,24},{24,28},{28,32},{32,36}... | collective-permute-start | bytes 227336 | tf_op jit(solution)/shard_map/ppermute | solution.py:280

commit v3 on v2

--- a/solution.py
+++ b/solution.py
@@ -9,11 +9,9 @@
 FIELDS = 3 * LEVELS + 2
 SCALE = 16.0
 SHIFTS = (8.0, 2.0, 20.0)
+FACTORS = (1.0, 2.0, 4.0, 1.0 / 3.0, 2.0 / 3.0, 5.0 / 3.0)
 F32 = jnp.float32
 VMEM = pltpu.VMEM
-
-MASS = {"s": 0.25, "d": 1.0 / 12.0}
-SLOPE = {"s": 0.0, "d": 1.0}
 
 
 def side_kernel(src_ref, eta_ref, fric_ref, mask_ref, fields_ref, low_ref, high_ref, mask, sems):
@@ -60,15 +58,7 @@
     return pltpu.roll(value, 1, axis)
 
 
-def coefficient(mode, cx, cy, cz):
-    x, y, z = mode
-    total = cx * SLOPE[x] * MASS[y] * MASS[z]
-    total += cy * MASS[x] * SLOPE[y] * MASS[z]
-    return total + cz * MASS[x] * MASS[y] * SLOPE[z]
-
-
-def flat_modes(plane):
-    after = ahead(plane, 1)
+def flat_modes(plane, after):
     s, d = plane + after, after - plane
     s1, d1 = ahead(s, 0), ahead(d, 0)
     return {"ss": s + s1, "ds": s1 - s, "sd": d + d1, "dd": d1 - d}
@@ -77,10 +67,11 @@
 def flat_back(modes):
     s = modes["ss"] - modes["ds"] + behind(modes["ss"] + modes["ds"], 0)
     d = modes["sd"] - modes["dd"] + behind(modes["sd"] + modes["dd"], 0)
-    return s - d + behind(s + d, 1)
+    return s - d, s + d
 
 
 def layer(lower, upper, eta):
+    whole, double, four, third, two_thirds, five_thirds = eta
     modes = []
     for c in (0, 1):
         m = {}
@@ -91,23 +82,21 @@
         modes.append(m)
     low, high = [], []
     for c in (0, 1):
-        weights = (4.0, 1.0, 4.0) if c == 0 else (1.0, 4.0, 4.0)
-        own, other = modes[c], modes[1 - c]
-        out = {}
-        for m, value in own.items():
-            out[m] = coefficient(m, *weights) * value
-        for z in "sd":
-            q = 0.25 * MASS[z]
-            double, single = ("ds", "sd") if c == 0 else ("sd", "ds")
-            out[double + z] = out[double + z] + (2.0 * q) * other[single + z]
-            out[single + z] = out[single + z] + q * other[double + z]
-        out = {m: value * eta for m, value in out.items()}
-        lo, hi = {}, {}
-        for xy in ("ss", "ds", "sd", "dd"):
-            d = out[xy + "d"]
-            s = out.get(xy + "s")
-            lo[xy] = -d if s is None else s - d
-            hi[xy] = d if s is None else s + d
+        u, v = modes[c], modes[1 - c]
+        first, second = ("ds", "sd") if c == 0 else ("sd", "ds")
+        up = {
+            first + "s": double * (u[first + "s"] + u[first + "s"] + v[second + "s"]),
+            second + "s": whole * (u[second + "s"] + v[first + "s"]),
+            first + "d": two_thirds * (4.0 * u[first + "d"] + v[second + "d"]),
+            second + "d": third * (5.0 * u[second + "d"] + v[first + "d"]),
+            "dds": five_thirds * u["dds"],
+            "ddd": whole * u["ddd"],
+        }
+        ssd = four * u["ssd"]
+        lo, hi = {"ss": -ssd}, {"ss": ssd}
+        for xy in ("ds", "sd", "dd"):
+            lo[xy] = up[xy + "s"] - up[xy + "d"]
+            hi[xy] = up[xy + "s"] + up[xy + "d"]
         low.append(lo)
         high.append(hi)
     return low, high
@@ -115,7 +104,7 @@
 
 def krylov_kernel(
     fields_ref, left_ref, right_ref, next_ref, prev_ref,
-    out_ref, row_ref, vec, cell, frict, mask,
+    out_ref, row_ref, vec, eta, cell, after, near, far, frict, mask,
 ):
     lane = lax.broadcasted_iota(jnp.int32, (16, 128), 1)
     left = jnp.concatenate([left_ref[...], next_ref[FIELDS + 1], prev_ref[FIELDS + 1]], 0)
@@ -128,42 +117,61 @@
         side = jnp.where(lane >= 125, from_left, jnp.where(lane < 3, from_right, zero))
         return jnp.concatenate([own, side], 1)
 
+    for l in range(LEVELS):
+        eta[l] = plane(2 * LEVELS + l)
+    mask[...] = plane(3 * LEVELS + 1)
     frict[...] = plane(3 * LEVELS) * (1.0 / SCALE)
-    mask_plane = plane(3 * LEVELS + 1)
-    mask[...] = mask_plane
     for l in range(LEVELS):
-        vec[0, 0, l] = plane(l) * mask_plane
-        vec[0, 1, l] = plane(LEVELS + l) * mask_plane
-    below = None
+        vec[0, 0, l] = plane(l)
+        vec[0, 1, l] = plane(LEVELS + l)
+    for l in range(LEVELS - 1):
+        value = (eta[l] + eta[l + 1]) * (0.125 / SCALE / 16.0)
+        cell[0, l] = value + ahead(value, 1)
+    for l in range(LEVELS - 1):
+        value = cell[0, l] + ahead(cell[0, l], 0)
+        for n, factor in enumerate(FACTORS):
+            cell[n, l] = factor * value
     for l in range(LEVELS):
-        value = plane(2 * LEVELS + l)
-        value = value + ahead(value, 1)
-        value = value + ahead(value, 0)
-        if below is not None:
-            cell[l - 1] = (below + value) * (0.125 / SCALE)
-        below = value
+        for c in (0, 1):
+            vec[0, c, l] = vec[0, c, l] * mask[...]
 
     for k in range(3):
         shift = SHIFTS[k] / SCALE
 
-        def finish(l, sums):
+        for c in (0, 1):
+            for l in range(LEVELS):
+                after[c, l] = ahead(vec[k, c, l], 1)
+        for side in (slice(0, 128), slice(128, 256)):
+            lower, pending = None, None
+            for l in range(LEVELS):
+                upper = [
+                    flat_modes(vec[k, c, l, :, side], after[c, l, :, side]) for c in (0, 1)
+                ]
+                if l:
+                    eta_parts = [cell[n, l - 1, :, side] for n in range(len(FACTORS))]
+                    sums, high = layer(lower, upper, eta_parts)
+                    if pending is not None:
+                        sums = [{m: sums[c][m] + pending[c][m] for m in sums[c]} for c in (0, 1)]
+                    for c in (0, 1):
+                        near[c, l - 1, :, side], far[c, l - 1, :, side] = flat_back(sums[c])
+                    pending = high
+                lower = upper
             for c in (0, 1):
-                value = vec[k, c, l]
-                image = flat_back(sums[c])
-                if l == 0:
-                    image = image + frict[...] * value
-                vec[k + 1, c, l] = image * mask[...] - shift * value
-
-        lower = [flat_modes(vec[k, c, 0]) for c in (0, 1)]
-        pending = None
-        for l in range(LEVELS - 1):
-            upper = [flat_modes(vec[k, c, l + 1]) for c in (0, 1)]
-            low, high = layer(lower, upper, cell[l])
-            if pending is not None:
-                low = [{m: low[c][m] + pending[c][m] for m in low[c]} for c in (0, 1)]
-            finish(l, low)
-            lower, pending = upper, high
-        finish(LEVELS - 1, pending)
+                near[c, LEVELS - 1, :, side], far[c, LEVELS - 1, :, side] = flat_back(pending[c])
+        for c in (0, 1):
+            for l in range(LEVELS):
+                if k < 2:
+                    image = near[c, l] + behind(far[c, l], 1)
+                    value = vec[k, c, l]
+                    if l == 0:
+                        image = image + frict[...] * value
+                    vec[k + 1, c, l] = image * mask[...] - shift * value
+                else:
+                    image = near[c, l, 0:8, 0:128] + behind(far[c, l, 0:8], 1)[:, 0:128]
+                    value = vec[k, c, l, 0:8, 0:128]
+                    if l == 0:
+                        image = image + frict[0:8, 0:128] * value
+                    vec[k + 1, c, l, 0:8, 0:128] = image * mask[0:8, 0:128] - shift * value
 
     pairs = ((0, 0), (0, 1), (0, 2), (1, 1), (1, 2), (2, 2), (1, 3), (2, 3))
     sums = [jnp.zeros((8, 128), F32) for _ in pairs]
@@ -273,17 +281,31 @@
         pltpu.SemaphoreType.DMA((5,)),
         space=pltpu.HBM,
     )(*[pltpu.with_memory_space_constraint(a, pltpu.HBM) for a in arguments])
-    left = lax.ppermute(high, gy, [(i, i + 1) for i in range(size_y - 1)])
-    right = lax.ppermute(low, gy, [(i + 1, i) for i in range(size_y - 1)])
+    odd_y = lax.axis_index(gy) % 2 == 1
+    middle = [(i, i + 1) for i in range(1, size_y - 1, 2)]
+    middle += [(b, a) for a, b in middle]
+    got_middle = lax.ppermute(jnp.where(odd_y, high, low), gy, middle)
+    got_pair = lax.ppermute(jnp.where(odd_y, low, high), gy, [(i, i ^ 1) for i in range(size_y)])
+    right = jnp.where(odd_y, got_middle, got_pair)
+    left = jnp.where(odd_y, got_pair, got_middle)
     down, up = call(rows_kernel, [shape(FIELDS + 2, 4, 128)] * 2, 2)(fields, right, left)
-    following = lax.ppermute(down, gx, [(i + 1, i) for i in range(size_x - 1)])
-    previous = lax.ppermute(up, gx, [(i, i + 1) for i in range(size_x - 1)])
+    odd = lax.axis_index(gx) % 2 == 1
+    outer = [(i, i + 1) for i in range(1, size_x - 1, 2)]
+    outer += [(b, a) for a, b in outer]
+    got_outer = lax.ppermute(jnp.where(odd, up, down), gx, outer)
+    got_inner = lax.ppermute(jnp.where(odd, down, up), gx, [(i, i ^ 1) for i in range(size_x)])
+    following = jnp.where(odd, got_outer, got_inner)
+    previous = jnp.where(odd, got_inner, got_outer)
     vectors, row = call(
         krylov_kernel,
         [shape(4, 2, LEVELS, 8, 128), shape(1, 128)],
         8,
         VMEM((4, 2, LEVELS, 16, 256), F32),
-        VMEM((LEVELS - 1, 16, 256), F32),
+        VMEM((LEVELS, 16, 256), F32),
+        VMEM((len(FACTORS), LEVELS - 1, 16, 256), F32),
+        VMEM((2, LEVELS, 16, 256), F32),
+        VMEM((2, LEVELS, 16, 256), F32),
+        VMEM((2, LEVELS, 16, 256), F32),
         VMEM((16, 256), F32),
         VMEM((16, 256), F32),
     )(fields, left, right, following, previous)

time: 69.3 us -> 66.4 us (0.958)
  blocking collectives: 39.3 us -> 36.5 us
  Pallas kernels: 6.43 us -> 4.5 us
  starting transfers between devices: 18.1 us -> 19.5 us
    all_to_all x2, blocking collectives: 39.3 us -> 36.5 us  [everywhere(): return lax.all_to_all(spread, axes, 0, 0, tiled=True)]
    pallas_call x4, Pallas kernels: 6.43 us -> 4.5 us  [run(): pl.pallas_call(kernel, out_shape=tuple(outs), in_specs=[pl.BlockSpec(memo...]
    ppermute x4, starting transfers between devices: 18.1 us -> 19.5 us  [the longest x1 10.5 us: local(): lax.ppermute(jnp.where(odd, down, up), gx, [(i, i ^ 1) for i in range(siz...]
where the time goes in v3:
time: 66.4 us; the launch traced here: 66.1 us
  blocking collectives  36.5 us (55%)
  starting transfers between devices  19.5 us (29%)
  waiting for transfers between devices  4.71 us (7%)
  Pallas kernels  4.5 us (7%)
  between operations  0.75 us (1%)
    all_to_all x2, blocking collectives, everywhere(): return lax.all_to_all(spread, axes, 0, 0, tiled=True)  36.5 us
    ppermute x1, starting transfers between devices, local(): lax.ppermute(jnp.where(odd, down, up), gx, [(i, i ^ 1) for i in range(siz...  10.5 us
    ppermute x1, starting transfers between devices, local(): lax.ppermute(jnp.where(odd_y, low, high), gy, [(i, i ^ 1) for i in range(...  6.41 us
    pallas_call x4, Pallas kernels, run(): pl.pallas_call(kernel, out_shape=tuple(outs), in_specs=[pl.BlockSpec(memo...  4.5 us
    ppermute x1, waiting for transfers between devices, local(): got_outer = lax.ppermute(jnp.where(odd, up, down), gx, outer)  3.76 us
    ppermute x1, starting transfers between devices, local(): got_outer = lax.ppermute(jnp.where(odd, up, down), gx, outer)  1.92 us
  transfers between devices with their start and end apart: 4, of which 2 were waited for; matrix products, arithmetic and copies ran while one was open for 0% of the time, Pallas kernels for 0%

profile of v3, /device:TPU:1, one launch (start us, length us, event | category | flops | bytes accessed | tf_op | source)
XLA Modules:
  0.0 66.1 jit_solution(7587361018316844070)
XLA Ops:
  0.6 1.0 %shard_map.59 = (f32[35,8,128]{2,1,0:T(8,128)S(1)}, f32[8,128]{1,0:T(8,128)S(1)}, f32[8,128]{1,0:T(8,128)S(1)}) custom-call(f32[2,11,8,128]{3,2,1,0:T(8,128)} %src_ref.1, f32[11,8,128]{2,1,0:T(8,128)} %eta_ref.1, f32[8,128]{1,0:T(8,128)} %fric_ref.1, s32[8,128]{1,0:T(8,128)} %mask_ref.1), custom_call_target="tpu_custom_call" | custom-call | tf_op jit(solution)/shard_map/pallas_call | solution.py:251
  1.7 0.7 %collective-permute-start.1 = (f32[8,128]{1,0:T(8,128)S(1)}, f32[8,128]{1,0:T(8,128)S(1)}, u32[]{:S(2)}, u32[]{:S(2)}) collective-permute-start(f32[8,128]{1,0:T(8,128)S(1)} %get-tuple-element.22), channel_id=1, source_target_pairs={{1,2},{2,1},{5,6},{6,5},{9,10},{10,9},{13,14},{14,13},{17,18},{18,... | collective-permute-start | bytes 12296 | tf_op jit(solution)/shard_map/ppermute | solution.py:287
  2.4 6.4 %collective-permute-start = (f32[8,128]{1,0:T(8,128)S(1)}, f32[8,128]{1,0:T(8,128)S(1)}, u32[]{:S(2)}, u32[]{:S(2)}) collective-permute-start(f32[8,128]{1,0:T(8,128)S(1)} %get-tuple-element.23), channel_id=1, source_target_pairs={{0,1},{1,0},{2,3},{3,2},{4,5},{5,4},{6,7},{7,6},{8,9},{9,8},{10,11... | collective-permute-start | bytes 12296 | tf_op jit(solution)/shard_map/ppermute | solution.py:288
  8.8 0.0 collective-permute-done.1
  8.8 0.9 %collective-permute-done = f32[8,128]{1,0:T(8,128)S(1)} collective-permute-done((f32[8,128]{1,0:T(8,128)S(1)}, f32[8,128]{1,0:T(8,128)S(1)}, u32[]{:S(2)}, u32[]{:S(2)}) %collective-permute-start) | collective-permute-done | bytes 4128 | tf_op jit(solution)/shard_map/ppermute | solution.py:288
  9.8 10.5 %collective-permute-start.3 = (f32[37,4,128]{2,1,0:T(4,128)S(1)}, f32[37,4,128]{2,1,0:T(4,128)S(1)}, u32[]{:S(2)}, u32[]{:S(2)}) collective-permute-start(f32[37,4,128]{2,1,0:T(4,128)S(1)} %get-tuple-element.18), channel_id=1, source_target_pairs={{0,4},{4,0},{8,12},{12,8},{16,20},{20,16},{24,28},{28,24},{32,36},... | collective-permute-start | bytes 227336 | tf_op jit(solution)/shard_map/ppermute | solution.py:296
  20.4 1.9 %collective-permute-start.2 = (f32[37,4,128]{2,1,0:T(4,128)S(1)}, f32[37,4,128]{2,1,0:T(4,128)S(1)}, u32[]{:S(2)}, u32[]{:S(2)}) collective-permute-start(f32[37,4,128]{2,1,0:T(4,128)S(1)} %get-tuple-element.19), channel_id=1, source_target_pairs={{4,8},{12,16},{20,24},{28,32},{36,40},{44,48},{52,56},{60,64},{68,... | collective-permute-start | bytes 227336 | tf_op jit(solution)/shard_map/ppermute | solution.py:295
  22.3 0.0 collective-permute-done.3
  22.3 3.8 %collective-permute-done.2 = f32[37,4,128]{2,1,0:T(4,128)S(1)} collective-permute-done((f32[37,4,128]{2,1,0:T(4,128)S(1)}, f32[37,4,128]{2,1,0:T(4,128)S(1)}, u32[]{:S(2)}, u32[]{:S(2)}) %collective-permute-start.2) | collective-permute-done | bytes 75808 | tf_op jit(solution)/shard_map/ppermute | solution.py:295
  26.1 2.6 %shard_map.61 = (f32[4,2,11,8,128]{4,3,2,1,0:T(8,128)S(1)}, f32[1,128]{1,0:T(1,128)S(1)}) custom-call(f32[35,8,128]{2,1,0:T(8,128)S(1)} %get-tuple-element.9.fields_ref, f32[8,128]{1,0:T(8,128)S(1)} %get-tuple-element.21.left_ref, f32[8,128]{1,0:T(8,128)S(1)} %get-tuple-element.20.right_ref, f32[37,4,128]{2,1,0:T(4,128)S(1)} %get-tuple-element.17.next_ref, ...), custom_call_target="tpu_custom_call" | custom-call | tf_op jit(solution)/shard_map/pallas_call | solution.py:251
  28.7 18.9 %all_to_all.10 = f32[24,1,128]{2,1,0:T(1,128)S(1)} all-to-all(f32[24,1,128]{2,1,0:T(1,128)S(1)} %broadcast_in_dim.7), channel_id=1, replica_groups=mesh['far'=8,'near'=24,'gy'=4] {'near'}, dimensions={0} | all-to-all | bytes 24576 | tf_op jit(solution)/shard_map/all_to_all | solution.py:270
  47.6 17.6 %all_to_all.11 = f32[32,1,128]{2,1,0:T(1,128)S(1)} all-to-all(f32[32,1,128]{2,1,0:T(1,128)S(1)} %broadcast_in_dim.16), channel_id=1, replica_groups=mesh['far'=8,'near'=24,'gy'=4] {'far','gy'}, dimensions={0} | all-to-all | bytes 32768 | tf_op jit(solution)/shard_map/all_to_all | solution.py:270
  65.3 0.9 %shard_map.62 = (f32[2,11,8,128]{3,2,1,0:T(8,128)}, f32[2,11,8,128]{3,2,1,0:T(8,128)}) custom-call(f32[4,2,11,8,128]{4,3,2,1,0:T(8,128)S(1)} %get-tuple-element.14.vec_ref, f32[32,128]{1,0:T(8,128)S(1)} %bitcast.3), custom_call_target="tpu_custom_call" | custom-call | tf_op jit(solution)/shard_map/pallas_call | solution.py:251
  (8 shorter events, 0.1 us)
Async XLA Ops:
  1.7 7.1 %collective-permute-start.1 = (f32[8,128]{1,0:T(8,128)S(1)}, f32[8,128]{1,0:T(8,128)S(1)}, u32[]{:S(2)}, u32[]{:S(2)}) collective-permute-start(f32[8,128]{1,0:T(8,128)S(1)} %get-tuple-element.22), channel_id=1, source_target_pairs={{1,2},{2,1},{5,6},{6,5},{9,10},{10,9},{13,14},{14,13},{17,18},{18,... | collective-permute-start | bytes 12296 | tf_op jit(solution)/shard_map/ppermute | solution.py:287
  2.4 7.4 %collective-permute-start = (f32[8,128]{1,0:T(8,128)S(1)}, f32[8,128]{1,0:T(8,128)S(1)}, u32[]{:S(2)}, u32[]{:S(2)}) collective-permute-start(f32[8,128]{1,0:T(8,128)S(1)} %get-tuple-element.23), channel_id=1, source_target_pairs={{0,1},{1,0},{2,3},{3,2},{4,5},{5,4},{6,7},{7,6},{8,9},{9,8},{10,11... | collective-permute-start | bytes 12296 | tf_op jit(solution)/shard_map/ppermute | solution.py:288
  9.8 12.5 %collective-permute-start.3 = (f32[37,4,128]{2,1,0:T(4,128)S(1)}, f32[37,4,128]{2,1,0:T(4,128)S(1)}, u32[]{:S(2)}, u32[]{:S(2)}) collective-permute-start(f32[37,4,128]{2,1,0:T(4,128)S(1)} %get-tuple-element.18), channel_id=1, source_target_pairs={{0,4},{4,0},{8,12},{12,8},{16,20},{20,16},{24,28},{28,24},{32,36},... | collective-permute-start | bytes 227336 | tf_op jit(solution)/shard_map/ppermute | solution.py:296
  20.4 5.7 %collective-permute-start.2 = (f32[37,4,128]{2,1,0:T(4,128)S(1)}, f32[37,4,128]{2,1,0:T(4,128)S(1)}, u32[]{:S(2)}, u32[]{:S(2)}) collective-permute-start(f32[37,4,128]{2,1,0:T(4,128)S(1)} %get-tuple-element.19), channel_id=1, source_target_pairs={{4,8},{12,16},{20,24},{28,32},{36,40},{44,48},{52,56},{60,64},{68,... | collective-permute-start | bytes 227336 | tf_op jit(solution)/shard_map/ppermute | solution.py:295

commit v4 on v3

--- a/solution.py
+++ b/solution.py
@@ -271,7 +271,7 @@
 
 
 def local(*arguments):
-    gx, gy = ("far", "near"), "gy"
+    gx, gy = ("far", "mid", "core"), "gy"
     size_x, size_y = lax.axis_size(gx), lax.axis_size(gy)
     fields, low, high = call(
         side_kernel,
@@ -285,7 +285,9 @@
     middle = [(i, i + 1) for i in range(1, size_y - 1, 2)]
     middle += [(b, a) for a, b in middle]
     got_middle = lax.ppermute(jnp.where(odd_y, high, low), gy, middle)
-    got_pair = lax.ppermute(jnp.where(odd_y, low, high), gy, [(i, i ^ 1) for i in range(size_y)])
+    duos = [[i, i + 1] for i in range(0, size_y, 2)]
+    duo = lax.all_gather(jnp.where(odd_y, low, high), gy, axis_index_groups=duos)
+    got_pair = jnp.where(odd_y, duo[0], duo[1])
     right = jnp.where(odd_y, got_middle, got_pair)
     left = jnp.where(odd_y, got_pair, got_middle)
     down, up = call(rows_kernel, [shape(FIELDS + 2, 4, 128)] * 2, 2)(fields, right, left)
@@ -293,9 +295,9 @@
     outer = [(i, i + 1) for i in range(1, size_x - 1, 2)]
     outer += [(b, a) for a, b in outer]
     got_outer = lax.ppermute(jnp.where(odd, up, down), gx, outer)
-    got_inner = lax.ppermute(jnp.where(odd, down, up), gx, [(i, i ^ 1) for i in range(size_x)])
-    following = jnp.where(odd, got_outer, got_inner)
-    previous = jnp.where(odd, got_inner, got_outer)
+    both = lax.all_gather(jnp.where(odd, down, up), "core")
+    following = jnp.where(odd, got_outer, both[1])
+    previous = jnp.where(odd, both[0], got_outer)
     vectors, row = call(
         krylov_kernel,
         [shape(4, 2, LEVELS, 8, 128), shape(1, 128)],
@@ -309,15 +311,15 @@
         VMEM((16, 256), F32),
         VMEM((16, 256), F32),
     )(fields, left, right, following, previous)
-    row = jnp.sum(everywhere(row, "near"), axis=0)
+    row = jnp.sum(everywhere(row, ("mid", "core")), axis=0)
     rows = everywhere(row, ("far", "gy"))[:, 0]
     return call(combine_kernel, [shape(2, LEVELS, 8, 128)] * 2, 4)(vectors, rows)
 
 
 def solution(mesh):
     size_x, size_y = mesh.devices.shape
-    split = Mesh(mesh.devices.reshape(8, size_x // 8, size_y), ("far", "near", "gy"))
-    gx = ("far", "near")
+    split = Mesh(mesh.devices.reshape(8, size_x // 16, 2, size_y), ("far", "mid", "core", "gy"))
+    gx = ("far", "mid", "core")
     vector, plane = P(None, None, gx, "gy"), P(gx, "gy")
     return jax.shard_map(
         local,

time: 66.4 us -> 62.1 us (0.935)
  blocking collectives: 36.5 us -> 50.1 us
  starting transfers between devices: 19.5 us -> 6.37 us
  waiting for transfers between devices: 4.71 us -> 0.01 us
    ppermute x2 -> x0, starting transfers between devices: 16.9 us -> none  [the longest x1 10.5 us: local(): lax.ppermute(jnp.where(odd, down, up), gx, [(i, i ^ 1) for i in range(siz...]
    all_gather x0 -> x2, blocking collectives: none -> 11.4 us  [the longest x1 6.2 us: local(): lax.all_gather(jnp.where(odd_y, low, high), gy, axis_index_groups=duos)]
    ppermute x1, starting transfers between devices: 1.92 us -> 5.71 us  [local(): got_outer = lax.ppermute(jnp.where(odd, up, down), gx, outer)]
    ppermute x1, waiting for transfers between devices: 3.76 us -> 0.01 us  [local(): got_outer = lax.ppermute(jnp.where(odd, up, down), gx, outer)]
    all_to_all x2, blocking collectives: 36.5 us -> 38.7 us  [everywhere(): return lax.all_to_all(spread, axes, 0, 0, tiled=True)]
    ppermute x2 -> x0, waiting for transfers between devices: 0.95 us -> none  [the longest x1 0.95 us: local(): lax.ppermute(jnp.where(odd_y, low, high), gy, [(i, i ^ 1) for i in range(...]
  transfers between devices with their start and end apart: 4 -> 2, of which waited for: 2 -> 0; matrix products, arithmetic and copies ran while one was open for 0% -> 0% of each run, Pallas kernels for 0% -> 0%
where the time goes in v4:
time: 62.1 us; the launch traced here: 61.8 us
  blocking collectives  50.1 us (81%)
  starting transfers between devices  6.37 us (10%)
  Pallas kernels  4.5 us (7%)
  between operations  0.73 us (1%)
    all_to_all x2, blocking collectives, everywhere(): return lax.all_to_all(spread, axes, 0, 0, tiled=True)  38.7 us
    all_gather x1, blocking collectives, local(): lax.all_gather(jnp.where(odd_y, low, high), gy, axis_index_groups=duos)  6.2 us
    ppermute x1, starting transfers between devices, local(): got_outer = lax.ppermute(jnp.where(odd, up, down), gx, outer)  5.71 us
    all_gather x1, blocking collectives, local(): both = lax.all_gather(jnp.where(odd, down, up), 'core')  5.17 us
    pallas_call x4, Pallas kernels, run(): pl.pallas_call(kernel, out_shape=tuple(outs), in_specs=[pl.BlockSpec(memo...  4.5 us
  transfers between devices with their start and end apart: 2, of which 0 were waited for; matrix products, arithmetic and copies ran while one was open for 0% of the time, Pallas kernels for 0%

profile of v4, /device:TPU:1, one launch (start us, length us, event | category | flops | bytes accessed | tf_op | source)
XLA Modules:
  0.0 61.8 jit_solution(14828215002603653080)
XLA Ops:
  0.6 1.0 %shard_map.59 = (f32[35,8,128]{2,1,0:T(8,128)S(1)}, f32[8,128]{1,0:T(8,128)S(1)}, f32[8,128]{1,0:T(8,128)S(1)}) custom-call(f32[2,11,8,128]{3,2,1,0:T(8,128)} %src_ref.1, f32[11,8,128]{2,1,0:T(8,128)} %eta_ref.1, f32[8,128]{1,0:T(8,128)} %fric_ref.1, s32[8,128]{1,0:T(8,128)} %mask_ref.1), custom_call_target="tpu_custom_call" | custom-call | tf_op jit(solution)/shard_map/pallas_call | solution.py:251
  1.7 0.7 %collective-permute-start = (f32[8,128]{1,0:T(8,128)S(1)}, f32[8,128]{1,0:T(8,128)S(1)}, u32[]{:S(2)}, u32[]{:S(2)}) collective-permute-start(f32[8,128]{1,0:T(8,128)S(1)} %get-tuple-element.23), channel_id=1, source_target_pairs={{1,2},{2,1},{5,6},{6,5},{9,10},{10,9},{13,14},{14,13},{17,18},{18,... | collective-permute-start | bytes 12296 | tf_op jit(solution)/shard_map/ppermute | solution.py:287
  2.4 6.2 %all-gather = f32[16,128]{1,0:T(8,128)S(1)} all-gather(f32[8,128]{1,0:T(8,128)S(1)} %get-tuple-element.22), channel_id=2, replica_groups={{0,1},{2,3},{4,5},{6,7},{8,9},{10,11},{12,13},{14,15},{16,17},{18,19},{..., dimensions={0}, use_global_device_ids=true | all-gather | bytes 12288 | tf_op jit(solution)/shard_map/all_gather | solution.py:289
  8.6 0.0 collective-permute-done
  8.7 5.7 %collective-permute-start.1 = (f32[37,4,128]{2,1,0:T(4,128)S(1)}, f32[37,4,128]{2,1,0:T(4,128)S(1)}, u32[]{:S(2)}, u32[]{:S(2)}) collective-permute-start(f32[37,4,128]{2,1,0:T(4,128)S(1)} %get-tuple-element.19), channel_id=1, source_target_pairs={{4,8},{12,16},{20,24},{28,32},{36,40},{44,48},{52,56},{60,64},{68,... | collective-permute-start | bytes 227336 | tf_op jit(solution)/shard_map/ppermute | solution.py:297
  14.4 5.2 %all-gather.1 = f32[74,4,128]{2,1,0:T(4,128)S(1)} all-gather(f32[37,4,128]{2,1,0:T(4,128)S(1)} %get-tuple-element.18), channel_id=3, replica_groups=mesh['far'=8,'mid'=12,'core'=2,'gy'=4] {'core'}, dimensions={0}, use_global_device_ids=true | all-gather | bytes 227328 | tf_op jit(solution)/shard_map/all_gather | solution.py:298
  19.5 0.0 collective-permute-done.1
  19.6 2.6 %shard_map.61 = (f32[4,2,11,8,128]{4,3,2,1,0:T(8,128)S(1)}, f32[1,128]{1,0:T(1,128)S(1)}) custom-call(f32[35,8,128]{2,1,0:T(8,128)S(1)} %get-tuple-element.9.fields_ref, f32[8,128]{1,0:T(8,128)S(1)} %get-tuple-element.21.left_ref, f32[8,128]{1,0:T(8,128)S(1)} %get-tuple-element.20.right_ref, f32[37,4,128]{2,1,0:T(4,128)S(1)} %get-tuple-element.17.next_ref, ...), custom_call_target="tpu_custom_call" | custom-call | tf_op jit(solution)/shard_map/pallas_call | solution.py:251
  22.2 21.0 %all_to_all.10 = f32[24,1,128]{2,1,0:T(1,128)S(1)} all-to-all(f32[24,1,128]{2,1,0:T(1,128)S(1)} %broadcast_in_dim.7), channel_id=1, replica_groups=mesh['far'=8,'mid'=12,'core'=2,'gy'=4] {'mid','core'}, dimensions={0} | all-to-all | bytes 24576 | tf_op jit(solution)/shard_map/all_to_all | solution.py:270
  43.2 17.7 %all_to_all.11 = f32[32,1,128]{2,1,0:T(1,128)S(1)} all-to-all(f32[32,1,128]{2,1,0:T(1,128)S(1)} %broadcast_in_dim.16), channel_id=1, replica_groups=mesh['far'=8,'mid'=12,'core'=2,'gy'=4] {'far','gy'}, dimensions={0} | all-to-all | bytes 32768 | tf_op jit(solution)/shard_map/all_to_all | solution.py:270
  60.9 0.9 %shard_map.62 = (f32[2,11,8,128]{3,2,1,0:T(8,128)}, f32[2,11,8,128]{3,2,1,0:T(8,128)}) custom-call(f32[4,2,11,8,128]{4,3,2,1,0:T(8,128)S(1)} %get-tuple-element.14.vec_ref, f32[32,128]{1,0:T(8,128)S(1)} %bitcast.3), custom_call_target="tpu_custom_call" | custom-call | tf_op jit(solution)/shard_map/pallas_call | solution.py:251
  (8 shorter events, 0.1 us)
Async XLA Ops:
  1.7 6.9 %collective-permute-start = (f32[8,128]{1,0:T(8,128)S(1)}, f32[8,128]{1,0:T(8,128)S(1)}, u32[]{:S(2)}, u32[]{:S(2)}) collective-permute-start(f32[8,128]{1,0:T(8,128)S(1)} %get-tuple-element.23), channel_id=1, source_target_pairs={{1,2},{2,1},{5,6},{6,5},{9,10},{10,9},{13,14},{14,13},{17,18},{18,... | collective-permute-start | bytes 12296 | tf_op jit(solution)/shard_map/ppermute | solution.py:287
  8.7 10.9 %collective-permute-start.1 = (f32[37,4,128]{2,1,0:T(4,128)S(1)}, f32[37,4,128]{2,1,0:T(4,128)S(1)}, u32[]{:S(2)}, u32[]{:S(2)}) collective-permute-start(f32[37,4,128]{2,1,0:T(4,128)S(1)} %get-tuple-element.19), channel_id=1, source_target_pairs={{4,8},{12,16},{20,24},{28,32},{36,40},{44,48},{52,56},{60,64},{68,... | collective-permute-start | bytes 227336 | tf_op jit(solution)/shard_map/ppermute | solution.py:297

commit v5 on v4

--- a/solution.py
+++ b/solution.py
@@ -185,7 +185,7 @@
     totals = jnp.sum(stacked, axis=1, keepdims=True)
     ids = [lax.broadcasted_iota(jnp.int32, (8, 128), a) for a in (0, 1)]
     spread = jnp.where(ids[0] == ids[1], totals, 0.0)
-    row_ref[...] = jnp.sum(spread, axis=0, keepdims=True)
+    row_ref[...] = jnp.broadcast_to(jnp.sum(spread, axis=0, keepdims=True), (8, 128))
 
 
 def coordinates(gram):
@@ -290,7 +290,7 @@
     got_pair = jnp.where(odd_y, duo[0], duo[1])
     right = jnp.where(odd_y, got_middle, got_pair)
     left = jnp.where(odd_y, got_pair, got_middle)
-    down, up = call(rows_kernel, [shape(FIELDS + 2, 4, 128)] * 2, 2)(fields, right, left)
+    down, up = call(rows_kernel, [shape(FIELDS + 3, 4, 128)] * 2, 2)(fields, right, left)
     odd = lax.axis_index(gx) % 2 == 1
     outer = [(i, i + 1) for i in range(1, size_x - 1, 2)]
     outer += [(b, a) for a, b in outer]
@@ -300,7 +300,7 @@
     previous = jnp.where(odd, both[0], got_outer)
     vectors, row = call(
         krylov_kernel,
-        [shape(4, 2, LEVELS, 8, 128), shape(1, 128)],
+        [shape(4, 2, LEVELS, 8, 128), shape(8, 128)],
         8,
         VMEM((4, 2, LEVELS, 16, 256), F32),
         VMEM((LEVELS, 16, 256), F32),
@@ -311,7 +311,7 @@
         VMEM((16, 256), F32),
         VMEM((16, 256), F32),
     )(fields, left, right, following, previous)
-    row = jnp.sum(everywhere(row, ("mid", "core")), axis=0)
+    row = jnp.sum(everywhere(row[0:1], ("mid", "core")), axis=0)
     rows = everywhere(row, ("far", "gy"))[:, 0]
     return call(combine_kernel, [shape(2, LEVELS, 8, 128)] * 2, 4)(vectors, rows)
 

time: 62.1 us -> 62.1 us (level)
  no operation moved by 1% of the time
where the time goes in v5:
time: 62.1 us; the launch traced here: 61.8 us
  blocking collectives  50.1 us (81%)
  starting transfers between devices  6.37 us (10%)
  Pallas kernels  4.5 us (7%)
  between operations  0.72 us (1%)
    all_to_all x2, blocking collectives, everywhere(): return lax.all_to_all(spread, axes, 0, 0, tiled=True)  38.7 us
    all_gather x1, blocking collectives, local(): lax.all_gather(jnp.where(odd_y, low, high), gy, axis_index_groups=duos)  6.2 us
    ppermute x1, starting transfers between devices, local(): got_outer = lax.ppermute(jnp.where(odd, up, down), gx, outer)  5.71 us
    all_gather x1, blocking collectives, local(): both = lax.all_gather(jnp.where(odd, down, up), 'core')  5.18 us
    pallas_call x4, Pallas kernels, run(): pl.pallas_call(kernel, out_shape=tuple(outs), in_specs=[pl.BlockSpec(memo...  4.5 us
  transfers between devices with their start and end apart: 2, of which 0 were waited for; matrix products, arithmetic and copies ran while one was open for 0% of the time, Pallas kernels for 0%

profile of v5, /device:TPU:1, one launch (start us, length us, event | category | flops | bytes accessed | tf_op | source)
XLA Modules:
  0.0 61.8 jit_solution(5030050946043786898)
XLA Ops:
  0.6 1.0 %shard_map.59 = (f32[35,8,128]{2,1,0:T(8,128)S(1)}, f32[8,128]{1,0:T(8,128)S(1)}, f32[8,128]{1,0:T(8,128)S(1)}) custom-call(f32[2,11,8,128]{3,2,1,0:T(8,128)} %src_ref.1, f32[11,8,128]{2,1,0:T(8,128)} %eta_ref.1, f32[8,128]{1,0:T(8,128)} %fric_ref.1, s32[8,128]{1,0:T(8,128)} %mask_ref.1), custom_call_target="tpu_custom_call" | custom-call | tf_op jit(solution)/shard_map/pallas_call | solution.py:251
  1.7 0.7 %collective-permute-start = (f32[8,128]{1,0:T(8,128)S(1)}, f32[8,128]{1,0:T(8,128)S(1)}, u32[]{:S(2)}, u32[]{:S(2)}) collective-permute-start(f32[8,128]{1,0:T(8,128)S(1)} %get-tuple-element.23), channel_id=1, source_target_pairs={{1,2},{2,1},{5,6},{6,5},{9,10},{10,9},{13,14},{14,13},{17,18},{18,... | collective-permute-start | bytes 12296 | tf_op jit(solution)/shard_map/ppermute | solution.py:287
  2.4 6.2 %all-gather = f32[16,128]{1,0:T(8,128)S(1)} all-gather(f32[8,128]{1,0:T(8,128)S(1)} %get-tuple-element.22), channel_id=2, replica_groups={{0,1},{2,3},{4,5},{6,7},{8,9},{10,11},{12,13},{14,15},{16,17},{18,19},{..., dimensions={0}, use_global_device_ids=true | all-gather | bytes 12288 | tf_op jit(solution)/shard_map/all_gather | solution.py:289
  8.6 0.0 collective-permute-done
  8.6 5.7 %collective-permute-start.1 = (f32[38,4,128]{2,1,0:T(4,128)S(1)}, f32[38,4,128]{2,1,0:T(4,128)S(1)}, u32[]{:S(2)}, u32[]{:S(2)}) collective-permute-start(f32[38,4,128]{2,1,0:T(4,128)S(1)} %bitcast.12), channel_id=1, source_target_pairs={{4,8},{12,16},{20,24},{28,32},{36,40},{44,48},{52,56},{60,64},{68,... | collective-permute-start | bytes 233480 | tf_op jit(solution)/shard_map/ppermute | solution.py:297
  14.4 5.2 %all-gather.1 = f32[76,4,128]{2,1,0:T(4,128)S(1)} all-gather(f32[38,4,128]{2,1,0:T(4,128)S(1)} %bitcast.11), channel_id=3, replica_groups=mesh['far'=8,'mid'=12,'core'=2,'gy'=4] {'core'}, dimensions={0}, use_global_device_ids=true | all-gather | bytes 233472 | tf_op jit(solution)/shard_map/all_gather | solution.py:298
  19.5 0.0 collective-permute-done.1
  19.6 2.6 %shard_map.61 = (f32[4,2,11,8,128]{4,3,2,1,0:T(8,128)S(1)}, f32[8,128]{1,0:T(8,128)S(1)}) custom-call(f32[35,8,128]{2,1,0:T(8,128)S(1)} %get-tuple-element.9.fields_ref, f32[8,128]{1,0:T(8,128)S(1)} %get-tuple-element.21.left_ref, f32[8,128]{1,0:T(8,128)S(1)} %get-tuple-element.20.right_ref, f32[38,4,128]{2,1,0:T(4,128)S(1)} %get-tuple-element.17.next_ref, ...), custom_call_target="tpu_custom_call" | custom-call | tf_op jit(solution)/shard_map/pallas_call | solution.py:251
  22.2 21.1 %all_to_all.10 = f32[24,1,128]{2,1,0:T(1,128)S(1)} all-to-all(f32[24,1,128]{2,1,0:T(1,128)S(1)} %broadcast_in_dim.7), channel_id=1, replica_groups=mesh['far'=8,'mid'=12,'core'=2,'gy'=4] {'mid','core'}, dimensions={0} | all-to-all | bytes 24576 | tf_op jit(solution)/shard_map/all_to_all | solution.py:270
  43.3 17.7 %all_to_all.11 = f32[32,1,128]{2,1,0:T(1,128)S(1)} all-to-all(f32[32,1,128]{2,1,0:T(1,128)S(1)} %broadcast_in_dim.16), channel_id=1, replica_groups=mesh['far'=8,'mid'=12,'core'=2,'gy'=4] {'far','gy'}, dimensions={0} | all-to-all | bytes 32768 | tf_op jit(solution)/shard_map/all_to_all | solution.py:270
  60.9 0.9 %shard_map.62 = (f32[2,11,8,128]{3,2,1,0:T(8,128)}, f32[2,11,8,128]{3,2,1,0:T(8,128)}) custom-call(f32[4,2,11,8,128]{4,3,2,1,0:T(8,128)S(1)} %get-tuple-element.14.vec_ref, f32[32,128]{1,0:T(8,128)S(1)} %bitcast.10), custom_call_target="tpu_custom_call" | custom-call | tf_op jit(solution)/shard_map/pallas_call | solution.py:251
  (9 shorter events, 0.1 us)
Async XLA Ops:
  1.7 6.9 %collective-permute-start = (f32[8,128]{1,0:T(8,128)S(1)}, f32[8,128]{1,0:T(8,128)S(1)}, u32[]{:S(2)}, u32[]{:S(2)}) collective-permute-start(f32[8,128]{1,0:T(8,128)S(1)} %get-tuple-element.23), channel_id=1, source_target_pairs={{1,2},{2,1},{5,6},{6,5},{9,10},{10,9},{13,14},{14,13},{17,18},{18,... | collective-permute-start | bytes 12296 | tf_op jit(solution)/shard_map/ppermute | solution.py:287
  8.6 10.9 %collective-permute-start.1 = (f32[38,4,128]{2,1,0:T(4,128)S(1)}, f32[38,4,128]{2,1,0:T(4,128)S(1)}, u32[]{:S(2)}, u32[]{:S(2)}) collective-permute-start(f32[38,4,128]{2,1,0:T(4,128)S(1)} %bitcast.12), channel_id=1, source_target_pairs={{4,8},{12,16},{20,24},{28,32},{36,40},{44,48},{52,56},{60,64},{68,... | collective-permute-start | bytes 233480 | tf_op jit(solution)/shard_map/ppermute | solution.py:297

commit v6 on v5

--- a/solution.py
+++ b/solution.py
@@ -14,7 +14,9 @@
 VMEM = pltpu.VMEM
 
 
-def side_kernel(src_ref, eta_ref, fric_ref, mask_ref, fields_ref, low_ref, high_ref, mask, sems):
+def side_kernel(
+    src_ref, eta_ref, fric_ref, mask_ref, odd_y_ref, fields_ref, middle_ref, pair_ref, mask, sems
+):
     parts = [
         (src_ref.at[0], fields_ref.at[0:LEVELS]),
         (src_ref.at[1], fields_ref.at[LEVELS : 2 * LEVELS]),
@@ -36,18 +38,25 @@
         place = (lane >= 3 * f) & (lane < 3 * f + 3)
         low = jnp.where(place, pltpu.roll(value, 3 * f, 1) if f else value, low)
         high = jnp.where(place, pltpu.roll(value, (3 * f - 125) % 128, 1), high)
-    low_ref[...] = low
-    high_ref[...] = high
-
-
-def rows_kernel(fields_ref, right_ref, left_ref, down_ref, up_ref):
-    for f in range(FIELDS):
-        value = fields_ref[f]
-        down_ref[f] = value[0:4]
-        up_ref[f] = value[4:8]
-    for f, value in ((FIELDS, right_ref[...]), (FIELDS + 1, left_ref[...])):
-        down_ref[f] = value[0:4]
-        up_ref[f] = value[4:8]
+    odd_y = odd_y_ref[...] > 0
+    middle_ref[...] = jnp.where(odd_y, high, low)
+    pair_ref[...] = jnp.where(odd_y, low, high)
+
+
+def rows_kernel(
+    fields_ref, middle_ref, duo_ref, odd_y_ref, odd_ref, outer_ref, inner_ref, left_ref, right_ref
+):
+    odd_y = odd_y_ref[...] > 0
+    pair = jnp.where(odd_y, duo_ref[0], duo_ref[1])
+    right = jnp.where(odd_y, middle_ref[...], pair)
+    left = jnp.where(odd_y, pair, middle_ref[...])
+    left_ref[...] = left
+    right_ref[...] = right
+    odd = odd_ref[0:4] > 0
+    for f in range(FIELDS + 2):
+        value = fields_ref[f] if f < FIELDS else (right, left)[f - FIELDS]
+        outer_ref[f] = jnp.where(odd, value[4:8], value[0:4])
+        inner_ref[f] = jnp.where(odd, value[0:4], value[4:8])
 
 
 def ahead(value, axis):
@@ -103,14 +112,23 @@
 
 
 def krylov_kernel(
-    fields_ref, left_ref, right_ref, next_ref, prev_ref,
+    fields_ref, left_ref, right_ref, outer_ref, both_ref, odd_ref,
     out_ref, row_ref, vec, eta, cell, after, near, far, frict, mask,
 ):
     lane = lax.broadcasted_iota(jnp.int32, (16, 128), 1)
-    left = jnp.concatenate([left_ref[...], next_ref[FIELDS + 1], prev_ref[FIELDS + 1]], 0)
-    right = jnp.concatenate([right_ref[...], next_ref[FIELDS], prev_ref[FIELDS]], 0)
+    odd = odd_ref[0:4] > 0
+
+    def joined(own, f):
+        outside = outer_ref[f]
+        following = jnp.where(odd, outside, both_ref[1, f])
+        previous = jnp.where(odd, both_ref[0, f], outside)
+        return jnp.concatenate([own, following, previous], 0)
+
+    left = joined(left_ref[...], FIELDS + 1)
+    right = joined(right_ref[...], FIELDS)
+
     def plane(f):
-        own = jnp.concatenate([fields_ref[f], next_ref[f], prev_ref[f]], 0)
+        own = joined(fields_ref[f], f)
         from_left = pltpu.roll(left, (125 - 3 * f) % 128, 1)
         from_right = pltpu.roll(right, (-3 * f) % 128, 1) if f else right
         zero = jnp.zeros((16, 128), F32)
@@ -246,12 +264,15 @@
             )
 
 
-def call(kernel, outs, megabytes, *scratch, space=VMEM):
+def call(kernel, outs, megabytes, *scratch, spaces=()):
     def run(*args):
         return pl.pallas_call(
             kernel,
             out_shape=tuple(outs),
-            in_specs=[pl.BlockSpec(memory_space=space)] * len(args),
+            in_specs=[
+                pl.BlockSpec(memory_space=spaces[n] if n < len(spaces) else VMEM)
+                for n in range(len(args))
+            ],
             out_specs=tuple([pl.BlockSpec(memory_space=VMEM)] * len(outs)),
             scratch_shapes=list(scratch),
             compiler_params=pltpu.CompilerParams(vmem_limit_bytes=megabytes << 20),
@@ -273,31 +294,28 @@
 def local(*arguments):
     gx, gy = ("far", "mid", "core"), "gy"
     size_x, size_y = lax.axis_size(gx), lax.axis_size(gy)
-    fields, low, high = call(
+    odd_y = jnp.full((8, 128), lax.axis_index(gy) % 2, jnp.int32)
+    odd = jnp.full((8, 128), lax.axis_index("core"), jnp.int32)
+    fields, to_middle, to_pair = call(
         side_kernel,
         [shape(FIELDS, 8, 128), shape(8, 128), shape(8, 128)],
         2,
         VMEM((8, 128), jnp.int32),
         pltpu.SemaphoreType.DMA((5,)),
-        space=pltpu.HBM,
-    )(*[pltpu.with_memory_space_constraint(a, pltpu.HBM) for a in arguments])
-    odd_y = lax.axis_index(gy) % 2 == 1
+        spaces=[pltpu.HBM] * 4,
+    )(*[pltpu.with_memory_space_constraint(a, pltpu.HBM) for a in arguments], odd_y)
     middle = [(i, i + 1) for i in range(1, size_y - 1, 2)]
     middle += [(b, a) for a, b in middle]
-    got_middle = lax.ppermute(jnp.where(odd_y, high, low), gy, middle)
+    got_middle = lax.ppermute(to_middle, gy, middle)
     duos = [[i, i + 1] for i in range(0, size_y, 2)]
-    duo = lax.all_gather(jnp.where(odd_y, low, high), gy, axis_index_groups=duos)
-    got_pair = jnp.where(odd_y, duo[0], duo[1])
-    right = jnp.where(odd_y, got_middle, got_pair)
-    left = jnp.where(odd_y, got_pair, got_middle)
-    down, up = call(rows_kernel, [shape(FIELDS + 3, 4, 128)] * 2, 2)(fields, right, left)
-    odd = lax.axis_index(gx) % 2 == 1
+    duo = lax.all_gather(to_pair, gy, axis_index_groups=duos)
+    to_outer, to_inner, left, right = call(
+        rows_kernel, [shape(FIELDS + 3, 4, 128)] * 2 + [shape(8, 128)] * 2, 2
+    )(fields, got_middle, duo, odd_y, odd)
     outer = [(i, i + 1) for i in range(1, size_x - 1, 2)]
     outer += [(b, a) for a, b in outer]
-    got_outer = lax.ppermute(jnp.where(odd, up, down), gx, outer)
-    both = lax.all_gather(jnp.where(odd, down, up), "core")
-    following = jnp.where(odd, got_outer, both[1])
-    previous = jnp.where(odd, both[0], got_outer)
+    got_outer = lax.ppermute(to_outer, gx, outer)
+    both = lax.all_gather(to_inner, "core")
     vectors, row = call(
         krylov_kernel,
         [shape(4, 2, LEVELS, 8, 128), shape(8, 128)],
@@ -310,7 +328,7 @@
         VMEM((2, LEVELS, 16, 256), F32),
         VMEM((16, 256), F32),
         VMEM((16, 256), F32),
-    )(fields, left, right, following, previous)
+    )(fields, left, right, got_outer, both, odd)
     row = jnp.sum(everywhere(row[0:1], ("mid", "core")), axis=0)
     rows = everywhere(row, ("far", "gy"))[:, 0]
     return call(combine_kernel, [shape(2, LEVELS, 8, 128)] * 2, 4)(vectors, rows)

time: 62.1 us -> 62 us (level)
  no operation moved by 1% of the time
where the time goes in v6:
time: 62 us; the launch traced here: 61.7 us
  blocking collectives  50.1 us (81%)
  starting transfers between devices  6.37 us (10%)
  Pallas kernels  4.51 us (7%)
  between operations  0.69 us (1%)
    all_to_all x2, blocking collectives, everywhere(): return lax.all_to_all(spread, axes, 0, 0, tiled=True)  38.7 us
    all_gather x1, blocking collectives, local(): duo = lax.all_gather(to_pair, gy, axis_index_groups=duos)  6.2 us
    ppermute x1, starting transfers between devices, local(): got_outer = lax.ppermute(to_outer, gx, outer)  5.71 us
    all_gather x1, blocking collectives, local(): both = lax.all_gather(to_inner, 'core')  5.18 us
    pallas_call x4, Pallas kernels, run(): pl.pallas_call(kernel, out_shape=tuple(outs), in_specs=[pl.BlockSpec(memo...  4.51 us
  transfers between devices with their start and end apart: 2, of which 0 were waited for; matrix products, arithmetic and copies ran while one was open for 0% of the time, Pallas kernels for 0%

profile of v6, /device:TPU:1, one launch (start us, length us, event | category | flops | bytes accessed | tf_op | source)
XLA Modules:
  0.0 61.7 jit_solution(4915133099553106451)
XLA Ops:
  0.7 1.0 %shard_map.59 = (f32[35,8,128]{2,1,0:T(8,128)S(1)}, f32[8,128]{1,0:T(8,128)S(1)}, f32[8,128]{1,0:T(8,128)S(1)}) custom-call(f32[2,11,8,128]{3,2,1,0:T(8,128)} %src_ref.1, f32[11,8,128]{2,1,0:T(8,128)} %eta_ref.1, f32[8,128]{1,0:T(8,128)} %fric_ref.1, s32[8,128]{1,0:T(8,128)} %mask_ref.1, s32[8,128]{1,0:T(8,128)S(1)} %broadcast_in_dim.20.odd_y_ref), custom_call_target="tpu_custom_call" | custom-call | tf_op jit(solution)/shard_map/pallas_call | solution.py:269
  1.7 0.7 %collective-permute-start = (f32[8,128]{1,0:T(8,128)S(1)}, f32[8,128]{1,0:T(8,128)S(1)}, u32[]{:S(2)}, u32[]{:S(2)}) collective-permute-start(f32[8,128]{1,0:T(8,128)S(1)} %get-tuple-element.12), channel_id=1, source_target_pairs={{1,2},{2,1},{5,6},{6,5},{9,10},{10,9},{13,14},{14,13},{17,18},{18,... | collective-permute-start | bytes 12296 | tf_op jit(solution)/shard_map/ppermute | solution.py:309
  2.4 6.2 %all-gather = f32[16,128]{1,0:T(8,128)S(1)} all-gather(f32[8,128]{1,0:T(8,128)S(1)} %get-tuple-element.13), channel_id=2, replica_groups={{0,1},{2,3},{4,5},{6,7},{8,9},{10,11},{12,13},{14,15},{16,17},{18,19},{..., dimensions={0}, use_global_device_ids=true | all-gather | bytes 12288 | tf_op jit(solution)/shard_map/all_gather | solution.py:311
  8.6 0.0 collective-permute-done.middle_ref
  8.6 5.7 %collective-permute-start.1 = (f32[38,4,128]{2,1,0:T(4,128)S(1)}, f32[38,4,128]{2,1,0:T(4,128)S(1)}, u32[]{:S(2)}, u32[]{:S(2)}) collective-permute-start(f32[38,4,128]{2,1,0:T(4,128)S(1)} %get-tuple-element.16), channel_id=1, source_target_pairs={{4,8},{12,16},{20,24},{28,32},{36,40},{44,48},{52,56},{60,64},{68,... | collective-permute-start | bytes 233480 | tf_op jit(solution)/shard_map/ppermute | solution.py:317
  14.3 5.2 %all-gather.1 = f32[76,4,128]{2,1,0:T(4,128)S(1)} all-gather(f32[38,4,128]{2,1,0:T(4,128)S(1)} %get-tuple-element.17), channel_id=3, replica_groups=mesh['far'=8,'mid'=12,'core'=2,'gy'=4] {'core'}, dimensions={0}, use_global_device_ids=true | all-gather | bytes 233472 | tf_op jit(solution)/shard_map/all_gather | solution.py:318
  19.5 0.0 collective-permute-done.1.outer_ref
  19.5 2.6 %shard_map.61 = (f32[4,2,11,8,128]{4,3,2,1,0:T(8,128)S(1)}, f32[8,128]{1,0:T(8,128)S(1)}) custom-call(f32[35,8,128]{2,1,0:T(8,128)S(1)} %get-tuple-element.11.fields_ref, f32[8,128]{1,0:T(8,128)S(1)} %get-tuple-element.14.left_ref, f32[8,128]{1,0:T(8,128)S(1)} %get-tuple-element.15.right_ref, f32[38,4,128]{2,1,0:T(4,128)S(1)} %collective-permute-done.1.outer_ref, ...), custom_call_target="tpu_custom_call" | custom-call | tf_op jit(solution)/shard_map/pallas_call | solution.py:269
  22.1 21.1 %all_to_all.10 = f32[24,1,128]{2,1,0:T(1,128)S(1)} all-to-all(f32[24,1,128]{2,1,0:T(1,128)S(1)} %broadcast_in_dim.23), channel_id=1, replica_groups=mesh['far'=8,'mid'=12,'core'=2,'gy'=4] {'mid','core'}, dimensions={0} | all-to-all | bytes 24576 | tf_op jit(solution)/shard_map/all_to_all | solution.py:291
  43.2 17.7 %all_to_all.11 = f32[32,1,128]{2,1,0:T(1,128)S(1)} all-to-all(f32[32,1,128]{2,1,0:T(1,128)S(1)} %broadcast_in_dim.24), channel_id=1, replica_groups=mesh['far'=8,'mid'=12,'core'=2,'gy'=4] {'far','gy'}, dimensions={0} | all-to-all | bytes 32768 | tf_op jit(solution)/shard_map/all_to_all | solution.py:291
  60.8 0.9 %shard_map.62 = (f32[2,11,8,128]{3,2,1,0:T(8,128)}, f32[2,11,8,128]{3,2,1,0:T(8,128)}) custom-call(f32[4,2,11,8,128]{4,3,2,1,0:T(8,128)S(1)} %get-tuple-element.18.vec_ref, f32[32,128]{1,0:T(8,128)S(1)} %bitcast.7), custom_call_target="tpu_custom_call" | custom-call | tf_op jit(solution)/shard_map/pallas_call | solution.py:269
  (7 shorter events, 0.1 us)
Async XLA Ops:
  1.7 6.9 %collective-permute-start = (f32[8,128]{1,0:T(8,128)S(1)}, f32[8,128]{1,0:T(8,128)S(1)}, u32[]{:S(2)}, u32[]{:S(2)}) collective-permute-start(f32[8,128]{1,0:T(8,128)S(1)} %get-tuple-element.12), channel_id=1, source_target_pairs={{1,2},{2,1},{5,6},{6,5},{9,10},{10,9},{13,14},{14,13},{17,18},{18,... | collective-permute-start | bytes 12296 | tf_op jit(solution)/shard_map/ppermute | solution.py:309
  8.6 10.9 %collective-permute-start.1 = (f32[38,4,128]{2,1,0:T(4,128)S(1)}, f32[38,4,128]{2,1,0:T(4,128)S(1)}, u32[]{:S(2)}, u32[]{:S(2)}) collective-permute-start(f32[38,4,128]{2,1,0:T(4,128)S(1)} %get-tuple-element.16), channel_id=1, source_target_pairs={{4,8},{12,16},{20,24},{28,32},{36,40},{44,48},{52,56},{60,64},{68,... | collective-permute-start | bytes 233480 | tf_op jit(solution)/shard_map/ppermute | solution.py:317

commit v7 on v6

--- a/solution.py
+++ b/solution.py
@@ -73,9 +73,10 @@
     return {"ss": s + s1, "ds": s1 - s, "sd": d + d1, "dd": d1 - d}
 
 
-def flat_back(modes):
+def flat_back(modes, rows):
     s = modes["ss"] - modes["ds"] + behind(modes["ss"] + modes["ds"], 0)
     d = modes["sd"] - modes["dd"] + behind(modes["sd"] + modes["dd"], 0)
+    s, d = s[rows], d[rows]
     return s - d, s + d
 
 
@@ -155,6 +156,7 @@
 
     for k in range(3):
         shift = SHIFTS[k] / SCALE
+        rows = slice(0, 16 if k < 2 else 8)
 
         for c in (0, 1):
             for l in range(LEVELS):
@@ -171,11 +173,15 @@
                     if pending is not None:
                         sums = [{m: sums[c][m] + pending[c][m] for m in sums[c]} for c in (0, 1)]
                     for c in (0, 1):
-                        near[c, l - 1, :, side], far[c, l - 1, :, side] = flat_back(sums[c])
+                        near[c, l - 1, rows, side], far[c, l - 1, rows, side] = flat_back(
+                            sums[c], rows
+                        )
                     pending = high
                 lower = upper
             for c in (0, 1):
-                near[c, LEVELS - 1, :, side], far[c, LEVELS - 1, :, side] = flat_back(pending[c])
+                near[c, LEVELS - 1, rows, side], far[c, LEVELS - 1, rows, side] = flat_back(
+                    pending[c], rows
+                )
         for c in (0, 1):
             for l in range(LEVELS):
                 if k < 2:
@@ -206,14 +212,20 @@
     row_ref[...] = jnp.broadcast_to(jnp.sum(spread, axis=0, keepdims=True), (8, 128))
 
 
+def tree(terms):
+    while len(terms) > 1:
+        pairs = [a + b for a, b in zip(terms[::2], terms[1::2])]
+        terms = pairs + terms[2 * len(pairs) :]
+    return terms[0]
+
+
 def coordinates(gram):
     def dot(a, b):
-        total = None
+        rows = []
         for i in range(len(a)):
-            for j in range(len(b)):
-                term = a[i] * b[j] * gram[min(i, j), max(i, j)]
-                total = term if total is None else total + term
-        return total
+            terms = [b[j] * gram[min(i, j), max(i, j)] for j in range(len(b))]
+            rows.append(a[i] * tree(terms))
+        return tree(rows)
 
     def added(a, b, factor):
         size = max(len(a), len(b))

time: 62 us -> 62 us (level)
  no operation moved by 1% of the time
where the time goes in v7:
time: 62 us; the launch traced here: 61.7 us
  blocking collectives  50.1 us (81%)
  starting transfers between devices  6.37 us (10%)
  Pallas kernels  4.5 us (7%)
  between operations  0.69 us (1%)
    all_to_all x2, blocking collectives, everywhere(): return lax.all_to_all(spread, axes, 0, 0, tiled=True)  38.7 us
    all_gather x1, blocking collectives, local(): duo = lax.all_gather(to_pair, gy, axis_index_groups=duos)  6.2 us
    ppermute x1, starting transfers between devices, local(): got_outer = lax.ppermute(to_outer, gx, outer)  5.71 us
    all_gather x1, blocking collectives, local(): both = lax.all_gather(to_inner, 'core')  5.18 us
    pallas_call x4, Pallas kernels, run(): pl.pallas_call(kernel, out_shape=tuple(outs), in_specs=[pl.BlockSpec(memo...  4.5 us
  transfers between devices with their start and end apart: 2, of which 0 were waited for; matrix products, arithmetic and copies ran while one was open for 0% of the time, Pallas kernels for 0%

profile of v7, /device:TPU:1, one launch (start us, length us, event | category | flops | bytes accessed | tf_op | source)
XLA Modules:
  0.0 61.7 jit_solution(15090899537627674936)
XLA Ops:
  0.7 1.0 %shard_map.59 = (f32[35,8,128]{2,1,0:T(8,128)S(1)}, f32[8,128]{1,0:T(8,128)S(1)}, f32[8,128]{1,0:T(8,128)S(1)}) custom-call(f32[2,11,8,128]{3,2,1,0:T(8,128)} %src_ref.1, f32[11,8,128]{2,1,0:T(8,128)} %eta_ref.1, f32[8,128]{1,0:T(8,128)} %fric_ref.1, s32[8,128]{1,0:T(8,128)} %mask_ref.1, s32[8,128]{1,0:T(8,128)S(1)} %broadcast_in_dim.20.odd_y_ref), custom_call_target="tpu_custom_call" | custom-call | tf_op jit(solution)/shard_map/pallas_call | solution.py:281
  1.7 0.7 %collective-permute-start = (f32[8,128]{1,0:T(8,128)S(1)}, f32[8,128]{1,0:T(8,128)S(1)}, u32[]{:S(2)}, u32[]{:S(2)}) collective-permute-start(f32[8,128]{1,0:T(8,128)S(1)} %get-tuple-element.12), channel_id=1, source_target_pairs={{1,2},{2,1},{5,6},{6,5},{9,10},{10,9},{13,14},{14,13},{17,18},{18,... | collective-permute-start | bytes 12296 | tf_op jit(solution)/shard_map/ppermute | solution.py:321
  2.4 6.2 %all-gather = f32[16,128]{1,0:T(8,128)S(1)} all-gather(f32[8,128]{1,0:T(8,128)S(1)} %get-tuple-element.13), channel_id=2, replica_groups={{0,1},{2,3},{4,5},{6,7},{8,9},{10,11},{12,13},{14,15},{16,17},{18,19},{..., dimensions={0}, use_global_device_ids=true | all-gather | bytes 12288 | tf_op jit(solution)/shard_map/all_gather | solution.py:323
  8.6 0.0 collective-permute-done.middle_ref
  8.6 5.7 %collective-permute-start.1 = (f32[38,4,128]{2,1,0:T(4,128)S(1)}, f32[38,4,128]{2,1,0:T(4,128)S(1)}, u32[]{:S(2)}, u32[]{:S(2)}) collective-permute-start(f32[38,4,128]{2,1,0:T(4,128)S(1)} %get-tuple-element.16), channel_id=1, source_target_pairs={{4,8},{12,16},{20,24},{28,32},{36,40},{44,48},{52,56},{60,64},{68,... | collective-permute-start | bytes 233480 | tf_op jit(solution)/shard_map/ppermute | solution.py:329
  14.3 5.2 %all-gather.1 = f32[76,4,128]{2,1,0:T(4,128)S(1)} all-gather(f32[38,4,128]{2,1,0:T(4,128)S(1)} %get-tuple-element.17), channel_id=3, replica_groups=mesh['far'=8,'mid'=12,'core'=2,'gy'=4] {'core'}, dimensions={0}, use_global_device_ids=true | all-gather | bytes 233472 | tf_op jit(solution)/shard_map/all_gather | solution.py:330
  19.5 0.0 collective-permute-done.1.outer_ref
  19.5 2.6 %shard_map.61 = (f32[4,2,11,8,128]{4,3,2,1,0:T(8,128)S(1)}, f32[8,128]{1,0:T(8,128)S(1)}) custom-call(f32[35,8,128]{2,1,0:T(8,128)S(1)} %get-tuple-element.11.fields_ref, f32[8,128]{1,0:T(8,128)S(1)} %get-tuple-element.14.left_ref, f32[8,128]{1,0:T(8,128)S(1)} %get-tuple-element.15.right_ref, f32[38,4,128]{2,1,0:T(4,128)S(1)} %collective-permute-done.1.outer_ref, ...), custom_call_target="tpu_custom_call" | custom-call | tf_op jit(solution)/shard_map/pallas_call | solution.py:281
  22.1 21.1 %all_to_all.10 = f32[24,1,128]{2,1,0:T(1,128)S(1)} all-to-all(f32[24,1,128]{2,1,0:T(1,128)S(1)} %broadcast_in_dim.23), channel_id=1, replica_groups=mesh['far'=8,'mid'=12,'core'=2,'gy'=4] {'mid','core'}, dimensions={0} | all-to-all | bytes 24576 | tf_op jit(solution)/shard_map/all_to_all | solution.py:303
  43.2 17.7 %all_to_all.11 = f32[32,1,128]{2,1,0:T(1,128)S(1)} all-to-all(f32[32,1,128]{2,1,0:T(1,128)S(1)} %broadcast_in_dim.24), channel_id=1, replica_groups=mesh['far'=8,'mid'=12,'core'=2,'gy'=4] {'far','gy'}, dimensions={0} | all-to-all | bytes 32768 | tf_op jit(solution)/shard_map/all_to_all | solution.py:303
  60.8 0.9 %shard_map.62 = (f32[2,11,8,128]{3,2,1,0:T(8,128)}, f32[2,11,8,128]{3,2,1,0:T(8,128)}) custom-call(f32[4,2,11,8,128]{4,3,2,1,0:T(8,128)S(1)} %get-tuple-element.18.vec_ref, f32[32,128]{1,0:T(8,128)S(1)} %bitcast.7), custom_call_target="tpu_custom_call" | custom-call | tf_op jit(solution)/shard_map/pallas_call | solution.py:281
  (7 shorter events, 0.1 us)
Async XLA Ops:
  1.7 6.9 %collective-permute-start = (f32[8,128]{1,0:T(8,128)S(1)}, f32[8,128]{1,0:T(8,128)S(1)}, u32[]{:S(2)}, u32[]{:S(2)}) collective-permute-start(f32[8,128]{1,0:T(8,128)S(1)} %get-tuple-element.12), channel_id=1, source_target_pairs={{1,2},{2,1},{5,6},{6,5},{9,10},{10,9},{13,14},{14,13},{17,18},{18,... | collective-permute-start | bytes 12296 | tf_op jit(solution)/shard_map/ppermute | solution.py:321
  8.6 10.9 %collective-permute-start.1 = (f32[38,4,128]{2,1,0:T(4,128)S(1)}, f32[38,4,128]{2,1,0:T(4,128)S(1)}, u32[]{:S(2)}, u32[]{:S(2)}) collective-permute-start(f32[38,4,128]{2,1,0:T(4,128)S(1)} %get-tuple-element.16), channel_id=1, source_target_pairs={{4,8},{12,16},{20,24},{28,32},{36,40},{44,48},{52,56},{60,64},{68,... | collective-permute-start | bytes 233480 | tf_op jit(solution)/shard_map/ppermute | solution.py:329

commit v8 on v7

--- a/solution.py
+++ b/solution.py
@@ -195,15 +195,16 @@
                     value = vec[k, c, l, 0:8, 0:128]
                     if l == 0:
                         image = image + frict[0:8, 0:128] * value
-                    vec[k + 1, c, l, 0:8, 0:128] = image * mask[0:8, 0:128] - shift * value
+                    out_ref[3, c, l] = image * mask[0:8, 0:128] - shift * value
 
     pairs = ((0, 0), (0, 1), (0, 2), (1, 1), (1, 2), (2, 2), (1, 3), (2, 3))
     sums = [jnp.zeros((8, 128), F32) for _ in pairs]
     for c in (0, 1):
         for l in range(LEVELS):
-            v = [vec[k, c, l, 0:8, 0:128] for k in range(4)]
-            for k in range(4):
+            v = [vec[k, c, l, 0:8, 0:128] for k in range(3)]
+            for k in range(3):
                 out_ref[k, c, l] = v[k]
+            v.append(out_ref[3, c, l])
             sums = [s + v[i] * v[j] for s, (i, j) in zip(sums, pairs)]
     stacked = jnp.concatenate([jnp.sum(s, axis=0, keepdims=True) for s in sums], 0)
     totals = jnp.sum(stacked, axis=1, keepdims=True)
@@ -332,7 +333,7 @@
         krylov_kernel,
         [shape(4, 2, LEVELS, 8, 128), shape(8, 128)],
         8,
-        VMEM((4, 2, LEVELS, 16, 256), F32),
+        VMEM((3, 2, LEVELS, 16, 256), F32),
         VMEM((LEVELS, 16, 256), F32),
         VMEM((len(FACTORS), LEVELS - 1, 16, 256), F32),
         VMEM((2, LEVELS, 16, 256), F32),

time: 62 us -> 62 us (level)
  no operation moved by 1% of the time
where the time goes in v8:
time: 62 us; the launch traced here: 61.7 us
  blocking collectives  50.1 us (81%)
  starting transfers between devices  6.37 us (10%)
  Pallas kernels  4.5 us (7%)
  between operations  0.69 us (1%)
    all_to_all x2, blocking collectives, everywhere(): return lax.all_to_all(spread, axes, 0, 0, tiled=True)  38.7 us
    all_gather x1, blocking collectives, local(): duo = lax.all_gather(to_pair, gy, axis_index_groups=duos)  6.2 us
    ppermute x1, starting transfers between devices, local(): got_outer = lax.ppermute(to_outer, gx, outer)  5.71 us
    all_gather x1, blocking collectives, local(): both = lax.all_gather(to_inner, 'core')  5.18 us
    pallas_call x4, Pallas kernels, run(): pl.pallas_call(kernel, out_shape=tuple(outs), in_specs=[pl.BlockSpec(memo...  4.5 us
  transfers between devices with their start and end apart: 2, of which 0 were waited for; matrix products, arithmetic and copies ran while one was open for 0% of the time, Pallas kernels for 0%

profile of v8, /device:TPU:1, one launch (start us, length us, event | category | flops | bytes accessed | tf_op | source)
XLA Modules:
  0.0 61.7 jit_solution(12007270631566313)
XLA Ops:
  0.7 1.0 %shard_map.59 = (f32[35,8,128]{2,1,0:T(8,128)S(1)}, f32[8,128]{1,0:T(8,128)S(1)}, f32[8,128]{1,0:T(8,128)S(1)}) custom-call(f32[2,11,8,128]{3,2,1,0:T(8,128)} %src_ref.1, f32[11,8,128]{2,1,0:T(8,128)} %eta_ref.1, f32[8,128]{1,0:T(8,128)} %fric_ref.1, s32[8,128]{1,0:T(8,128)} %mask_ref.1, s32[8,128]{1,0:T(8,128)S(1)} %broadcast_in_dim.20.odd_y_ref), custom_call_target="tpu_custom_call" | custom-call | tf_op jit(solution)/shard_map/pallas_call | solution.py:282
  1.7 0.7 %collective-permute-start = (f32[8,128]{1,0:T(8,128)S(1)}, f32[8,128]{1,0:T(8,128)S(1)}, u32[]{:S(2)}, u32[]{:S(2)}) collective-permute-start(f32[8,128]{1,0:T(8,128)S(1)} %get-tuple-element.12), channel_id=1, source_target_pairs={{1,2},{2,1},{5,6},{6,5},{9,10},{10,9},{13,14},{14,13},{17,18},{18,... | collective-permute-start | bytes 12296 | tf_op jit(solution)/shard_map/ppermute | solution.py:322
  2.4 6.2 %all-gather = f32[16,128]{1,0:T(8,128)S(1)} all-gather(f32[8,128]{1,0:T(8,128)S(1)} %get-tuple-element.13), channel_id=2, replica_groups={{0,1},{2,3},{4,5},{6,7},{8,9},{10,11},{12,13},{14,15},{16,17},{18,19},{..., dimensions={0}, use_global_device_ids=true | all-gather | bytes 12288 | tf_op jit(solution)/shard_map/all_gather | solution.py:324
  8.6 0.0 collective-permute-done.middle_ref
  8.6 5.7 %collective-permute-start.1 = (f32[38,4,128]{2,1,0:T(4,128)S(1)}, f32[38,4,128]{2,1,0:T(4,128)S(1)}, u32[]{:S(2)}, u32[]{:S(2)}) collective-permute-start(f32[38,4,128]{2,1,0:T(4,128)S(1)} %get-tuple-element.16), channel_id=1, source_target_pairs={{4,8},{12,16},{20,24},{28,32},{36,40},{44,48},{52,56},{60,64},{68,... | collective-permute-start | bytes 233480 | tf_op jit(solution)/shard_map/ppermute | solution.py:330
  14.3 5.2 %all-gather.1 = f32[76,4,128]{2,1,0:T(4,128)S(1)} all-gather(f32[38,4,128]{2,1,0:T(4,128)S(1)} %get-tuple-element.17), channel_id=3, replica_groups=mesh['far'=8,'mid'=12,'core'=2,'gy'=4] {'core'}, dimensions={0}, use_global_device_ids=true | all-gather | bytes 233472 | tf_op jit(solution)/shard_map/all_gather | solution.py:331
  19.5 0.0 collective-permute-done.1.outer_ref
  19.5 2.6 %shard_map.61 = (f32[4,2,11,8,128]{4,3,2,1,0:T(8,128)S(1)}, f32[8,128]{1,0:T(8,128)S(1)}) custom-call(f32[35,8,128]{2,1,0:T(8,128)S(1)} %get-tuple-element.11.fields_ref, f32[8,128]{1,0:T(8,128)S(1)} %get-tuple-element.14.left_ref, f32[8,128]{1,0:T(8,128)S(1)} %get-tuple-element.15.right_ref, f32[38,4,128]{2,1,0:T(4,128)S(1)} %collective-permute-done.1.outer_ref, ...), custom_call_target="tpu_custom_call" | custom-call | tf_op jit(solution)/shard_map/pallas_call | solution.py:282
  22.1 21.1 %all_to_all.10 = f32[24,1,128]{2,1,0:T(1,128)S(1)} all-to-all(f32[24,1,128]{2,1,0:T(1,128)S(1)} %broadcast_in_dim.23), channel_id=1, replica_groups=mesh['far'=8,'mid'=12,'core'=2,'gy'=4] {'mid','core'}, dimensions={0} | all-to-all | bytes 24576 | tf_op jit(solution)/shard_map/all_to_all | solution.py:304
  43.2 17.7 %all_to_all.11 = f32[32,1,128]{2,1,0:T(1,128)S(1)} all-to-all(f32[32,1,128]{2,1,0:T(1,128)S(1)} %broadcast_in_dim.24), channel_id=1, replica_groups=mesh['far'=8,'mid'=12,'core'=2,'gy'=4] {'far','gy'}, dimensions={0} | all-to-all | bytes 32768 | tf_op jit(solution)/shard_map/all_to_all | solution.py:304
  60.8 0.9 %shard_map.62 = (f32[2,11,8,128]{3,2,1,0:T(8,128)}, f32[2,11,8,128]{3,2,1,0:T(8,128)}) custom-call(f32[4,2,11,8,128]{4,3,2,1,0:T(8,128)S(1)} %get-tuple-element.18.vec_ref, f32[32,128]{1,0:T(8,128)S(1)} %bitcast.7), custom_call_target="tpu_custom_call" | custom-call | tf_op jit(solution)/shard_map/pallas_call | solution.py:282
  (7 shorter events, 0.1 us)
Async XLA Ops:
  1.7 6.9 %collective-permute-start = (f32[8,128]{1,0:T(8,128)S(1)}, f32[8,128]{1,0:T(8,128)S(1)}, u32[]{:S(2)}, u32[]{:S(2)}) collective-permute-start(f32[8,128]{1,0:T(8,128)S(1)} %get-tuple-element.12), channel_id=1, source_target_pairs={{1,2},{2,1},{5,6},{6,5},{9,10},{10,9},{13,14},{14,13},{17,18},{18,... | collective-permute-start | bytes 12296 | tf_op jit(solution)/shard_map/ppermute | solution.py:322
  8.6 10.9 %collective-permute-start.1 = (f32[38,4,128]{2,1,0:T(4,128)S(1)}, f32[38,4,128]{2,1,0:T(4,128)S(1)}, u32[]{:S(2)}, u32[]{:S(2)}) collective-permute-start(f32[38,4,128]{2,1,0:T(4,128)S(1)} %get-tuple-element.16), channel_id=1, source_target_pairs={{4,8},{12,16},{20,24},{28,32},{36,40},{44,48},{52,56},{60,64},{68,... | collective-permute-start | bytes 233480 | tf_op jit(solution)/shard_map/ppermute | solution.py:330
